TPU v7x, 32 devices: a whole 2x2x4 slice. The times are simulated.
32 devices in a mesh: grp: 2 (over y), slab: 4 (over z), blk: 2 (over x), sub: 2 (over core).
Axes of the slice: x: 2, y: 2, z: 4, core: 2. Of those that a mesh axis runs over, the one named last changes fastest.
Arguments:
- cell_x: int32 [8192], P(('grp', 'slab', 'blk', 'sub')), parts along dimension 0, may hold values from 0 to 63
- cell_y: int32 [8192], P(('grp', 'slab', 'blk', 'sub')), parts along dimension 0, may hold values from 0 to 127
- cell_z: int32 [8192], P(('grp', 'slab', 'blk', 'sub')), parts along dimension 0, may hold values from 0 to 127
- offsets: float32 [3, 8192], P(None, ('grp', 'slab', 'blk', 'sub')), parts along dimension 1, may hold values from 0 to 1
- charge: float32 [8192], P(('grp', 'slab', 'blk', 'sub')), parts along dimension 0, may hold values from -4 to 4
- block_count: int32 [32], P(('grp', 'slab', 'blk', 'sub')), parts along dimension 0, may hold values from 0 to 256, as said below
- level_amplitude: float32 [4], replicated, may hold values from 0.5 to 2
- density: float32 [512, 256, 256], P(('grp', 'slab'), 'blk', 'sub'), parts along dimension 0, may hold values from 0.3 to 8.2
Outputs:
- field: float32 [512, 256, 256], P(('grp', 'slab'), 'blk', 'sub'), parts along dimension 0
- energy: float32 [2], P('grp'), parts along dimension 0
There are 2 independent parts, one for each index of `grp`. A program takes and returns all parts, laid end to end along the dimension named above; an argument that names none is the same for every part. Nothing has to cross between parts.
Inputs may be any that keep to these rules, and one draw needn't show every extreme that they name: `block_count`: within the 1 block of each device, blocks with a nonzero count come before blocks with count 0; some device has every block full.
All inputs are finite; a program needn't handle non-finite values.
Results may differ from a plain program's by a relative error of at most 0.0021.
Values sent between devices are 32-bit elements; how exact they have to be, the bound alone decides.
No kernel may reach another device: no remote copies, remote signals or barrier semaphores. Data moves between devices by JAX's collectives and lax.ppermute only.
A program may use at most 64 MiB of HBM per device.

v0:
```python
import math
from fractions import Fraction

import jax
import jax.numpy as jnp
from jax import lax
from jax.experimental import pallas as pl
from jax.experimental.pallas import tpu as pltpu
from jax.sharding import PartitionSpec as P

G0X = 64
G0Y = 128
G0Z = 128
BQ = 256
LEVELS = 4
GROUPS = ((0, 1), (2, 3))

spread_width = 1.25
exponent = -0.5 / spread_width**2 * math.log2(math.e)

vmem = pl.BlockSpec(memory_space=pltpu.VMEM)
smem = pl.BlockSpec(memory_space=pltpu.SMEM)
hbm = pl.BlockSpec(memory_space=pltpu.HBM)
params = pltpu.CompilerParams(vmem_limit_bytes=48 * 2**20)


def round_up(value, unit):
    return -(-value // unit) * unit


class Plan:
    def __init__(self, fine, rows):
        self.rows = rows
        self.dims = [
            tuple(base * (LEVELS - level) // LEVELS for base in (G0X, G0Y, G0Z))
            for level in range(LEVELS)
        ]
        self.cells = [
            tuple(dim * part // whole for dim, part, whole in zip(dims, rows, fine))
            for dims in self.dims
        ]
        self.nodes_x = [cells[0] + 1 for cells in self.cells]
        self.main_y = [round_up(cells[1], 16) for cells in self.cells]
        self.pad_x = [round_up(cells[0] + 1, 8) for cells in self.cells]
        self.pad_y = [
            max(main, round_up(cells[1] + 1, 8))
            for main, cells in zip(self.main_y, self.cells)
        ]
        self.pad_z = [round_up(cells[2] + 1, 8) for cells in self.cells]
        self.off_x = [sum(self.pad_x[:level]) for level in range(LEVELS + 1)]
        self.off_y = [sum(self.pad_y[:level]) for level in range(LEVELS + 1)]
        self.off_main = [0]
        for level in range(LEVELS):
            self.off_main.append(
                self.off_main[-1] + self.nodes_x[level] * self.main_y[level]
            )
        self.main_rows = self.off_main[-1]
        self.edge_rows = [
            round_up(self.pad_x[a] + self.pad_x[b], 16) for a, b in GROUPS
        ]
        self.off_edge = []
        at = self.main_rows
        for (a, b), count in zip(GROUPS, self.edge_rows):
            self.off_edge += [at, at + self.pad_x[a]]
            at += count
        self.total = at
        self.off_z = [0, self.pad_z[0], 0, self.pad_z[2]]
        self.width = max(
            round_up(self.pad_z[a] + self.pad_z[b], 128) for a, b in GROUPS
        )
        self.off_stack = [sum(self.main_y[:level]) for level in range(LEVELS + 1)]
        self.stack = round_up(self.off_stack[-1] + 8, 16)

    def main(self, level, node=0, count=1):
        pad = self.main_y[level]
        first = self.off_main[level] + node * pad
        return slice(first, first + count * pad)


def split(value):
    high = value.astype(jnp.bfloat16)
    return high, (value - high.astype(jnp.float32)).astype(jnp.bfloat16)


def dot(left, right, transposed=False):
    return lax.dot_general(
        left,
        right,
        (((1,), (1 if transposed else 0,)), ((), ())),
        preferred_element_type=jnp.float32,
    )


def hat(shape, fine_dim, rows, cells, shift, last):
    point = lax.broadcasted_iota(jnp.int32, shape, fine_dim)
    node = lax.broadcasted_iota(jnp.int32, shape, 1 - fine_dim) - shift
    apart = (node * rows - point * cells).astype(jnp.float32) / rows
    value = jnp.maximum(0.0, 1.0 - jnp.abs(apart))
    return jnp.where((node >= 0) & (node <= last), value, 0.0)


def edge_hat(plan, shape, row_dim):
    row = lax.broadcasted_iota(jnp.int32, shape, row_dim)
    column = lax.broadcasted_iota(jnp.int32, shape, 1 - row_dim)
    value = jnp.zeros(shape, jnp.float32)
    for level in range(LEVELS):
        cells = plan.cells[level][0]
        node = column - (plan.off_edge[level] - plan.main_rows)
        apart = (node * plan.rows[0] - (row >> 3) * cells).astype(jnp.float32)
        one = jnp.maximum(0.0, 1.0 - jnp.abs(apart / plan.rows[0]))
        here = ((row & 7) == level) & (node >= 0) & (node <= cells)
        value = jnp.where(here, one, value)
    return value


def hats_kernel(plan, hat_y, hat_y_turned, hat_z, hat_z_turned, hat_x, hat_x_turned):
    _, rows_y, rows_z = plan.rows
    for turned in (False, True):
        fine_dim = 1 if turned else 0
        parts = []
        edge = 0.0
        for level in range(LEVELS):
            cells = plan.cells[level]
            shape = (rows_y, plan.main_y[level])
            parts.append(
                hat(
                    shape[::-1] if turned else shape, fine_dim, rows_y, cells[1], 0, cells[1] - 1
                )
            )
            shape = (rows_y, plan.stack - plan.off_stack[-1])
            shape = shape[::-1] if turned else shape
            one = hat(shape, fine_dim, rows_y, cells[1], level - cells[1], cells[1])
            column = lax.broadcasted_iota(jnp.int32, shape, 1 - fine_dim)
            edge = edge + jnp.where(column == level, one, 0.0)
            shape = (rows_z, plan.width)
            one = hat(
                shape[::-1] if not turned else shape,
                0 if turned else 1,
                rows_z,
                cells[2],
                plan.off_z[level],
                cells[2],
            ).astype(jnp.bfloat16)
            (hat_z_turned if turned else hat_z)[level] = jnp.concatenate([one, one], axis=0)
        whole = jnp.concatenate(parts + [edge], axis=1 - fine_dim).astype(jnp.bfloat16)
        if turned:
            hat_y_turned[...] = jnp.concatenate([whole, whole], axis=1)
        else:
            hat_y[...] = whole
    hat_x[...] = edge_hat(plan, hat_x.shape, 0).astype(jnp.bfloat16)
    hat_x_turned[...] = edge_hat(plan, hat_x_turned.shape, 1).astype(jnp.bfloat16)


def prepare_kernel(
    cell_x, cell_y, cell_z, offsets, charge, counts, amplitude, mine, scales,
    cells, shifts, held, levels, live, sems,
):
    blocks = mine.shape[0]
    copies = [
        pltpu.make_async_copy(source, target, sems.at[number])
        for number, (source, target) in enumerate(
            [
                (cell_x, cells.at[0]),
                (cell_y, cells.at[1]),
                (cell_z, cells.at[2]),
                (offsets, shifts),
                (charge, held),
                (counts, live),
                (amplitude, levels),
            ]
        )
    ]
    for copy in copies:
        copy.start()
    for copy in copies:
        copy.wait()
    slot = lax.broadcasted_iota(jnp.int32, (1, BQ), 1)
    for block in range(blocks):
        columns = slice(block * BQ, (block + 1) * BQ)
        mine[block, 0:1] = jnp.where(slot < live[block], held[:, columns], 0.0)
        for axis in range(3):
            mine[block, axis + 1 : axis + 2] = (
                cells[axis, :, columns].astype(jnp.float32) + shifts[axis : axis + 1, columns]
            )
    for level in range(LEVELS):
        scales[level : level + 1] = jnp.full((1, scales.shape[1]), levels[level], jnp.float32)
    scales[LEVELS:] = jnp.zeros((8 - LEVELS, scales.shape[1]), jnp.float32)


def weights(position, first, dim, base, rows):
    place = position * (dim / base)
    nodes = first + lax.broadcasted_iota(jnp.int32, (rows, 1), 0).astype(jnp.float32)
    apart = jnp.abs(nodes - place)
    apart = jnp.minimum(apart, dim - apart)
    return jnp.exp2(apart * apart * exponent)


def spread_kernel(plan, together, first, last, *refs):
    refs = list(refs)
    starts, charges = refs[:2]
    before = None if first else refs[2]
    turned = refs[2 if first else 3] if last else None
    outs = refs[2 + (not first) + last :]
    if last:
        energy = outs.pop(1)
    grids, along_x, along_y, along_z, planes = outs
    begin = [starts[axis].astype(jnp.float32) for axis in range(3)]
    steps = charges.shape[0] // together

    def one_step(step, before):
        for number in range(together):
            block = charges[step * together + number]
            columns = slice(number * BQ, (number + 1) * BQ)
            weighted, place_x, place_y, place_z = (block[row : row + 1] for row in range(4))
            for group, levels in enumerate(GROUPS):
                column_z = []
                for level in levels:
                    dims, cells = plan.dims[level], plan.cells[level]
                    along_x[plan.off_x[level] : plan.off_x[level + 1]] = weighted * weights(
                        place_x, begin[0] * cells[0], dims[0], G0X, plan.pad_x[level]
                    )
                    along_y[plan.off_y[level] : plan.off_y[level + 1]] = weights(
                        place_y, begin[1] * cells[1], dims[1], G0Y, plan.pad_y[level]
                    )
                    column_z.append(
                        weights(place_z, begin[2] * cells[2], dims[2], G0Z, plan.pad_z[level])
                    )
                rest = plan.width - sum(plan.pad_z[level] for level in levels)
                if rest:
                    column_z.append(jnp.zeros((rest, BQ), jnp.float32))
                along_z[group, :, columns] = jnp.concatenate(column_z, axis=0).astype(jnp.bfloat16)
                edges = []
                for level in levels:
                    fixed = along_y[plan.off_y[level] : plan.off_y[level] + plan.main_y[level]]
                    for node in range(plan.nodes_x[level]):
                        at = plan.off_x[level] + node
                        planes[plan.main(level, node), columns] = (
                            along_x[at : at + 1] * fixed
                        ).astype(jnp.bfloat16)
                    at = plan.off_y[level] + plan.cells[level][1]
                    edges.append(
                        along_x[plan.off_x[level] : plan.off_x[level + 1]] * along_y[at : at + 1]
                    )
                rest = plan.edge_rows[group] - sum(edge.shape[0] for edge in edges)
                if rest:
                    edges.append(jnp.zeros((rest, BQ), jnp.float32))
                at = plan.off_edge[levels[0]]
                planes[at : at + plan.edge_rows[group], columns] = jnp.concatenate(
                    edges, axis=0
                ).astype(jnp.bfloat16)
        for group, levels in enumerate(GROUPS):
            at = plan.off_edge[levels[0]]
            for rows in [plan.main(level, 0, plan.nodes_x[level]) for level in levels] + [
                slice(at, at + plan.edge_rows[group])
            ]:
                value = dot(planes[rows], along_z[group], transposed=True)
                grids[rows] = value if before is None else before[rows] + value

    one_step(0, before)
    if steps <= 2:
        for step in range(1, steps):
            one_step(step, grids)
    else:
        lax.fori_loop(1, steps, lambda step, _: one_step(step, grids), None)
    if last:
        rows = plan.total // 8
        energy[...] = jnp.sum(
            (grids[...] * turned[...]).reshape(rows, 8, plan.width), axis=0
        )


def hat_terms(points, cells):
    terms = []
    for point in range(points):
        place = Fraction(point * cells, points)
        node = int(place)
        part = float(place - node)
        terms.append([(node, 1.0 - part)] + ([(node + 1, part)] if part else []))
    return terms


def turned_kernel(
    plan, density, scales, hat_y_turned, hat_z_turned, hat_x_turned, unused, out,
    held, along_y, along_x, sems,
):
    rows_x = plan.rows[0]
    parts = sems.shape[0]
    count = rows_x // parts
    copies = [
        pltpu.make_async_copy(
            density.at[pl.ds(part * count, count)],
            held.at[pl.ds(part * count, count)],
            sems.at[part],
        )
        for part in range(parts)
    ]
    for copy in copies:
        copy.start()
    terms = [hat_terms(rows_x, cells[0]) for cells in plan.cells]
    for part in range(parts):
        copies[part].wait()
        for plane in range(part * count, (part + 1) * count, 2):
            both = jnp.concatenate([held[plane], held[plane + 1]], axis=1)
            value = dot(hat_y_turned[...], jnp.concatenate(split(both), axis=0))
            along_y[plane] = value[:, : plan.rows[2]]
            along_y[plane + 1] = value[:, plan.rows[2] :]
    for level in range(LEVELS):
        stack = slice(plan.off_stack[level], plan.off_stack[level + 1])
        for node in range(plan.nodes_x[level]):
            total = None
            for plane in range(rows_x):
                for at, part in terms[level][plane]:
                    if at == node:
                        value = along_y[plane, stack]
                        if part != 1.0:
                            value = value * part
                        total = value if total is None else total + value
            if total is None:
                total = jnp.zeros((plan.main_y[level], plan.rows[2]), jnp.float32)
            along_x[plan.main(level, node)] = total
    first = plan.off_stack[-1]
    edges = jnp.concatenate([along_y[plane, first : first + 8] for plane in range(rows_x)], axis=0)
    high, low = split(edges)
    along_x[plan.main_rows :] = dot(hat_x_turned[...], high) + dot(hat_x_turned[...], low)
    for level in range(LEVELS):
        edge = plan.off_edge[level]
        for rows in (
            plan.main(level, 0, plan.nodes_x[level]),
            slice(edge, edge + plan.pad_x[level]),
        ):
            value = jnp.concatenate(split(along_x[rows]), axis=1)
            out[rows] = dot(value, hat_z_turned[level]) * scales[level : level + 1, :1]
    for group, levels in enumerate(GROUPS):
        at = plan.off_edge[levels[1]] + plan.pad_x[levels[1]]
        end = plan.off_edge[levels[0]] + plan.edge_rows[group]
        if end > at:
            out[at:end] = jnp.zeros((end - at, plan.width), jnp.float32)


def field_kernel(plan, part, parts, *refs):
    grids, scales, hat_y, hat_z, hat_x = refs[:5]
    field, drawn = refs[-2:]
    rows_x = plan.rows[0]
    count = rows_x // parts
    planes = range(part * count, (part + 1) * count)
    terms = [hat_terms(rows_x, cells[0]) for cells in plan.cells]

    def interpolate_z(level, rows):
        value = jnp.concatenate(split(grids[rows] * scales[level : level + 1, : plan.width]), axis=1)
        drawn[rows] = dot(value, hat_z[level])

    for level in range(LEVELS):
        used = [node for plane in planes for node, _ in terms[level][plane]]
        interpolate_z(level, plan.main(level, min(used), max(used) - min(used) + 1))
        edge = plan.off_edge[level]
        interpolate_z(level, slice(edge, edge + plan.pad_x[level]))
    for group, levels in enumerate(GROUPS):
        at = plan.off_edge[levels[1]] + plan.pad_x[levels[1]]
        end = plan.off_edge[levels[0]] + plan.edge_rows[group]
        if end > at:
            drawn[at:end] = jnp.zeros((end - at, drawn.shape[1]), jnp.float32)
    high, low = split(drawn[plan.main_rows :])
    rows = slice(planes[0] * 8, (planes[-1] + 1) * 8)
    edges = dot(hat_x[rows], high) + dot(hat_x[rows], low)
    rest = plan.stack - plan.off_stack[-1] - 8
    for plane in planes[::2]:
        both = []
        for one in (plane, plane + 1):
            stack = []
            for level in range(LEVELS):
                total = None
                for node, weight in terms[level][one]:
                    value = drawn[plan.main(level, node)]
                    if weight != 1.0:
                        value = value * weight
                    total = value if total is None else total + value
                stack.append(total)
            at = (one - planes[0]) * 8
            stack.append(edges[at : at + 8])
            if rest:
                stack.append(jnp.zeros((rest, drawn.shape[1]), jnp.float32))
            both.append(jnp.concatenate(stack, axis=0))
        value = dot(hat_y[...], jnp.concatenate(both, axis=1).astype(jnp.bfloat16))
        field[plane - planes[0]] = value[:, : plan.rows[2]]
        field[plane + 1 - planes[0]] = value[:, plan.rows[2] :]


def rounds(order):
    for axis in order:
        peers = lax.axis_size(axis)
        by = 1
        while by < peers:
            yield axis, [(i, i ^ by) for i in range(peers)]
            by *= 2


def on_device(cell_x, cell_y, cell_z, offsets, charge, block_count, level_amplitude, density):
    blocks = block_count.shape[0]
    rows = density.shape
    axes = ("slab", "blk", "sub")
    plan = Plan(tuple(count * lax.axis_size(axis) for count, axis in zip(rows, axes)), rows)
    order = ("sub", "blk", "slab")
    steps = list(rounds(order))
    f32, bf16 = jnp.float32, jnp.bfloat16

    hats = pl.pallas_call(
        lambda *refs: hats_kernel(plan, *refs),
        out_shape=[
            jax.ShapeDtypeStruct(shape, bf16)
            for shape in (
                (rows[1], plan.stack),
                (plan.stack, 2 * rows[1]),
                (LEVELS, 2 * plan.width, rows[2]),
                (LEVELS, 2 * rows[2], plan.width),
                (rows[0] * 8, plan.total - plan.main_rows),
                (plan.total - plan.main_rows, rows[0] * 8),
            )
        ],
        out_specs=[vmem] * 6,
        compiler_params=params,
        name="hats",
    )()
    hat_y, hat_y_turned, hat_z, hat_z_turned, hat_x, hat_x_turned = hats

    slots = blocks * BQ
    mine, scales = pl.pallas_call(
        prepare_kernel,
        out_shape=[
            jax.ShapeDtypeStruct((blocks, 4, BQ), f32),
            jax.ShapeDtypeStruct((8, 128), f32),
        ],
        in_specs=[hbm] * 7,
        out_specs=[vmem] * 2,
        scratch_shapes=[
            pltpu.VMEM((3, 1, slots), jnp.int32),
            pltpu.VMEM((3, slots), f32),
            pltpu.VMEM((1, slots), f32),
            pltpu.SMEM((LEVELS,), f32),
            pltpu.SMEM((blocks,), jnp.int32),
            pltpu.SemaphoreType.DMA((7,)),
        ],
        compiler_params=params,
        name="prepare",
    )(
        cell_x.reshape(1, slots),
        cell_y.reshape(1, slots),
        cell_z.reshape(1, slots),
        offsets,
        charge.reshape(1, slots),
        block_count,
        level_amplitude,
    )

    starts = jnp.stack([lax.axis_index(axis) for axis in axes]).astype(jnp.int32)
    grid_shape = jax.ShapeDtypeStruct((plan.total, plan.width), f32)

    def spread(charges, before, turned):
        count = charges.shape[0]
        together = math.gcd(count, 4)
        deep = together * BQ
        first, last = before is None, turned is not None
        operands = [starts, charges] + [x for x in (before, turned) if x is not None]
        return pl.pallas_call(
            lambda *refs: spread_kernel(plan, together, first, last, *refs),
            out_shape=[grid_shape] + [jax.ShapeDtypeStruct((8, plan.width), f32)] * last,
            in_specs=[smem] + [vmem] * (len(operands) - 1),
            out_specs=[vmem] * (1 + last),
            scratch_shapes=[
                pltpu.VMEM((plan.off_x[-1], BQ), f32),
                pltpu.VMEM((plan.off_y[-1], BQ), f32),
                pltpu.VMEM((len(GROUPS), plan.width, deep), bf16),
                pltpu.VMEM((plan.total, deep), bf16),
            ],
            input_output_aliases={} if first else {2: 0},
            cost_estimate=pl.CostEstimate(
                flops=2 * plan.total * 256 * BQ * count, bytes_accessed=0, transcendentals=0
            ),
            compiler_params=params,
            name="spread",
        )(*operands)

    parts = math.gcd(4, rows[0] // 2)
    turned = None
    grids = None
    held = mine
    for number, (axis, pairs) in enumerate(steps):
        got = lax.ppermute(held, axis, pairs)
        held = jnp.concatenate([held, got], axis=0)
        if turned is None:
            turned = pl.pallas_call(
                lambda *refs: turned_kernel(plan, *refs),
                out_shape=grid_shape,
                in_specs=[hbm] + [vmem] * 5,
                out_specs=vmem,
                scratch_shapes=[
                    pltpu.VMEM(rows, f32),
                    pltpu.VMEM((rows[0], plan.stack, rows[2]), f32),
                    pltpu.VMEM((plan.total, rows[2]), f32),
                    pltpu.SemaphoreType.DMA((parts,)),
                ],
                cost_estimate=pl.CostEstimate(
                    flops=2 * 10**9, bytes_accessed=math.prod(rows) * 4, transcendentals=0
                ),
                compiler_params=params,
                name="turned",
            )(density, scales, hat_y_turned, hat_z_turned, hat_x_turned, held)
        new = held if number == 0 else got
        end = number == len(steps) - 1
        out = spread(new, grids, turned if end else None)
        grids = out[0]
    energy = out[1]

    count = rows[0] // parts
    field = None
    for number, (axis, pairs) in enumerate(steps):
        got = lax.ppermute(energy, axis, pairs)
        if number < parts:
            operands = [grids, scales, hat_y, hat_z, hat_x, energy]
            specs = [vmem] * len(operands)
            if field is not None:
                operands.append(field)
                specs.append(hbm)
            field = pl.pallas_call(
                lambda *refs, part=number: field_kernel(plan, part, parts, *refs),
                grid=(1,),
                out_shape=jax.ShapeDtypeStruct(rows, f32),
                in_specs=specs,
                out_specs=pl.BlockSpec(
                    (count, rows[1], rows[2]), lambda i, part=number: (part, 0, 0)
                ),
                scratch_shapes=[pltpu.VMEM((plan.total, rows[2]), f32)],
                input_output_aliases={} if field is None else {len(operands) - 1: 0},
                cost_estimate=pl.CostEstimate(
                    flops=10**9, bytes_accessed=math.prod(rows) * 4 // parts, transcendentals=0
                ),
                compiler_params=params,
                name="field",
            )(*operands)
        energy = energy + got
    fine = math.prod(count * lax.axis_size(axis) for count, axis in zip(rows, axes))
    energy = jnp.sum(energy.reshape(1, -1), axis=1) / fine
    return field, energy


def solution(mesh):
    split_all = ("grp", "slab", "blk", "sub")
    in_specs = (
        P(split_all),
        P(split_all),
        P(split_all),
        P(None, split_all),
        P(split_all),
        P(split_all),
        P(),
        P(("grp", "slab"), "blk", "sub"),
    )
    out_specs = (P(("grp", "slab"), "blk", "sub"), P("grp"))
    return jax.shard_map(
        on_device, mesh=mesh, in_specs=in_specs, out_specs=out_specs, check_vma=False
    )
```

profile of v0, /device:TPU:0, one launch (start us, length us, event | category | flops | bytes accessed | tf_op | source)
XLA Modules:
  0.0 44.4 jit_solution(14682388498196065413)
XLA Ops:
  1.3 0.0 copy-start
  1.3 0.7 %copy-done = f32[3,256]{1,0:T(4,128)S(1)} copy-done((f32[3,256]{1,0:T(4,128)S(1)}, f32[3,256]{1,0:T(4,128)}, u32[]{:S(2)}) %copy-start) | copy-done | bytes 3096
  2.0 0.0 copy-start.1
  2.0 0.7 %copy-done.1 = s32[256]{0:T(256)S(1)} copy-done((s32[256]{0:T(256)S(1)}, s32[256]{0:T(256)}, u32[]{:S(2)}) %copy-start.1) | copy-done | bytes 1048
  2.6 0.0 copy-start.2
  2.6 0.7 %copy-done.2 = s32[256]{0:T(256)S(1)} copy-done((s32[256]{0:T(256)S(1)}, s32[256]{0:T(256)}, u32[]{:S(2)}) %copy-start.2) | copy-done | bytes 1048
  3.3 0.0 copy-start.3
  3.3 0.7 %copy-done.3 = s32[256]{0:T(256)S(1)} copy-done((s32[256]{0:T(256)S(1)}, s32[256]{0:T(256)}, u32[]{:S(2)}) %copy-start.3) | copy-done | bytes 1048
  4.0 0.0 copy-start.4
  4.0 0.7 %copy-done.4 = f32[256]{0:T(256)S(1)} copy-done((f32[256]{0:T(256)S(1)}, f32[256]{0:T(256)}, u32[]{:S(2)}) %copy-start.4) | copy-done | bytes 1048
  4.7 0.0 copy-start.5
  4.7 0.7 %copy-done.5 = f32[4]{0:T(128)S(1)} copy-done((f32[4]{0:T(128)S(1)}, f32[4]{0:T(128)}, u32[]{:S(2)}) %copy-start.5) | copy-done | bytes 40
  5.3 0.6 %prepare.1 = (f32[1,4,256]{2,1,0:T(4,128)S(1)}, f32[8,128]{1,0:T(8,128)S(1)}) custom-call(s32[1,256]{1,0:T(1,128)S(1)} %bitcast.8, s32[1,256]{1,0:T(1,128)S(1)} %bitcast.9, s32[1,256]{1,0:T(1,128)S(1)} %bitcast.10, f32[3,256]{1,0:T(4,128)S(1)} %copy-done, f32[1,256]{1,0:T(1,128)S(1)} %bitcast.11, s32[1]{0:T(128)S(6)} %copy.23.counts, f32[4]{0:T(128)S(1)} %copy-done.5), custom_call_target="tpu_custom_call" | custom-call | tf_op jit(solution)/shard_map/prepare/pallas_call | solution.py:426
  6.0 0.5 %collective-permute-start = (f32[1,4,256]{2,1,0:T(4,128)S(1)}, f32[1,4,256]{2,1,0:T(4,128)S(1)}, u32[]{:S(2)}, u32[]{:S(2)}) collective-permute-start(f32[1,4,256]{2,1,0:T(4,128)S(1)} %get-tuple-element.12), channel_id=1, source_target_pairs={{0,1},{1,0},{2,3},{3,2},{4,5},{5,4},{6,7},{7,6},{8,9},{9,8},{10,11... | collective-permute-start | bytes 12296 | tf_op jit(solution)/shard_map/ppermute | solution.py:487
  6.5 0.1 pad_add_fusion.refs_0_
  6.6 0.8 %hats.1 = (bf16[128,176]{1,0:T(8,128)(2,1)S(1)}, bf16[176,256]{1,0:T(8,128)(2,1)S(1)}, bf16[4,256,128]{2,1,0:T(8,128)(2,1)S(1)}, bf16[4,256,128]{2,1,0:T(8,128)(...) custom-call(), custom_call_target="tpu_custom_call" | custom-call | tf_op jit(solution)/shard_map/hats/pallas_call | solution.py:406
  7.4 0.0 collective-permute-done
  7.4 2.7 %collective-permute-start.1 = (f32[2,4,256]{2,1,0:T(4,128)S(1)}, f32[2,4,256]{2,1,0:T(4,128)S(1)}, u32[]{:S(2)}, u32[]{:S(2)}) collective-permute-start(f32[2,4,256]{2,1,0:T(4,128)S(1)} %constant_dynamic-update-slice_fusion.refs_1_.refs_5_), channel_id=1, source_target_pairs={{0,2},{2,0},{1,3},{3,1},{4,6},{6,4},{5,7},{7,5},{8,10},{10,8},{9,1... | collective-permute-start | bytes 24584 | tf_op jit(solution)/shard_map/ppermute | solution.py:487
  10.2 0.0 copy-start.6
  10.2 2.2 %copy-done.6 = f32[64,128,128]{2,1,0:T(8,128)S(1)} copy-done((f32[64,128,128]{2,1,0:T(8,128)S(1)}, f32[64,128,128]{2,1,0:T(8,128)}, u32[]{:S(2)}) %copy-start.6) | copy-done | bytes 4194328
  12.3 2.5 %turned.1.refs_3_ = f32[2160,128]{1,0:T(8,128)S(1)} custom-call(f32[64,128,128]{2,1,0:T(8,128)S(1)} %copy-done.6, f32[8,128]{1,0:T(8,128)S(1)} %get-tuple-element.13.refs_1_, bf16[176,256]{1,0:T(8,128)(2,1)S(1)} %get-tuple-element.14.refs_2_, bf16[4,256,128]{2,1,0:T(8,128)(2,1)S(1)} %get-tuple-element.15.refs_3_, ...), custom_call_target="tpu_custom_call" | custom-call | flops 2000000000 | bytes 4194304 | tf_op jit(solution)/shard_map/turned/pallas_call | solution.py:490
  14.8 1.4 %spread.4.refs_2_ = f32[2160,128]{1,0:T(8,128)S(1)} custom-call(s32[3]{0:T(128)S(1)} %pad_add_fusion.refs_0_, f32[2,4,256]{2,1,0:T(4,128)S(1)} %constant_dynamic-update-slice_fusion.refs_1_.refs_5_), custom_call_target="tpu_custom_call" | custom-call | flops 566231040 | tf_op jit(solution)/shard_map/spread/pallas_call | solution.py:463
  16.2 0.0 collective-permute-done.1.refs_1_
  16.3 1.6 %collective-permute-start.2 = (f32[4,4,256]{2,1,0:T(4,128)S(1)}, f32[4,4,256]{2,1,0:T(4,128)S(1)}, u32[]{:S(2)}, u32[]{:S(2)}) collective-permute-start(f32[4,4,256]{2,1,0:T(4,128)S(1)} %pad_maximum_fusion.1), channel_id=1, source_target_pairs={{0,4},{4,0},{8,12},{12,8},{1,5},{5,1},{9,13},{13,9},{2,6},{6,2},{1... | collective-permute-start | bytes 49160 | tf_op jit(solution)/shard_map/ppermute | solution.py:487
  17.9 1.5 %spread.5.refs_2_ = f32[2160,128]{1,0:T(8,128)S(1)} custom-call(s32[3]{0:T(128)S(1)} %pad_add_fusion.refs_0_, f32[2,4,256]{2,1,0:T(4,128)S(1)} %collective-permute-done.1.refs_1_, f32[2160,128]{1,0:T(8,128)S(1)} %spread.4.refs_2_), custom_call_target="tpu_custom_call", output_to_operand_aliasing={{}: (2, {})} | custom-call | flops 566231040 | tf_op jit(solution)/shard_map/spread/pallas_call | solution.py:463
  19.5 0.6 %collective-permute-done.2.refs_1_ = f32[4,4,256]{2,1,0:T(4,128)S(1)} collective-permute-done((f32[4,4,256]{2,1,0:T(4,128)S(1)}, f32[4,4,256]{2,1,0:T(4,128)S(1)}, u32[]{:S(2)}, u32[]{:S(2)}) %collective-permute-start.2) | collective-permute-done | bytes 16416 | tf_op jit(solution)/shard_map/ppermute | solution.py:487
  20.1 2.7 %collective-permute-start.3 = (f32[8,4,256]{2,1,0:T(4,128)S(1)}, f32[8,4,256]{2,1,0:T(4,128)S(1)}, u32[]{:S(2)}, u32[]{:S(2)}) collective-permute-start(f32[8,4,256]{2,1,0:T(4,128)S(1)} %pad_maximum_fusion), channel_id=1, source_target_pairs={{0,8},{4,12},{8,0},{12,4},{1,9},{5,13},{9,1},{13,5},{2,10},{6,14},... | collective-permute-start | bytes 98312 | tf_op jit(solution)/shard_map/ppermute | solution.py:487
  22.7 2.2 %spread.6.refs_2_ = f32[2160,128]{1,0:T(8,128)S(1)} custom-call(s32[3]{0:T(128)S(1)} %pad_add_fusion.refs_0_, f32[4,4,256]{2,1,0:T(4,128)S(1)} %collective-permute-done.2.refs_1_, f32[2160,128]{1,0:T(8,128)S(1)} %spread.5.refs_2_), custom_call_target="tpu_custom_call", output_to_operand_aliasing={{}: (2, {})} | custom-call | flops 1132462080 | tf_op jit(solution)/shard_map/spread/pallas_call | solution.py:463
  25.0 0.0 collective-permute-done.3.refs_1_
  25.0 3.6 %spread.7 = (f32[2160,128]{1,0:T(8,128)S(1)}, f32[8,128]{1,0:T(8,128)S(1)}) custom-call(s32[3]{0:T(128)S(1)} %pad_add_fusion.refs_0_, f32[8,4,256]{2,1,0:T(4,128)S(1)} %collective-permute-done.3.refs_1_, f32[2160,128]{1,0:T(8,128)S(1)} %spread.6.refs_2_, f32[2160,128]{1,0:T(8,128)S(1)} %turned.1.refs_3_), custom_call_target="tpu_custom_call", output_to_operand_aliasing={{0}: (2, {})} | custom-call | flops 2264924160 | tf_op jit(solution)/shard_map/spread/pallas_call | solution.py:463
  28.5 0.1 collective-permute-start.4
  28.6 1.6 %field.4.refs_6_ = f32[64,128,128]{2,1,0:T(8,128)} custom-call(f32[2160,128]{1,0:T(8,128)S(1)} %get-tuple-element.17.refs_0_, f32[8,128]{1,0:T(8,128)S(1)} %get-tuple-element.13.refs_1_, bf16[128,176]{1,0:T(8,128)(2,1)S(1)} %get-tuple-element.18.refs_2_, bf16[4,256,128]{2,1,0:T(8,128)(2,1)S(1)} %get-tuple-element.19.refs_3_, ...), custom_call_target="tpu_custom_call" | custom-call | flops 1000000000 | bytes 1048576 | tf_op jit(solution)/shard_map/field/pallas_call | solution.py:523
  30.3 0.0 collective-permute-done.4
  30.3 0.5 %collective-permute-start.5 = (f32[8,128]{1,0:T(8,128)S(1)}, f32[8,128]{1,0:T(8,128)S(1)}, u32[]{:S(2)}, u32[]{:S(2)}) collective-permute-start(f32[8,128]{1,0:T(8,128)S(1)} %add.12.refs_5_), channel_id=1, source_target_pairs={{0,2},{2,0},{1,3},{3,1},{4,6},{6,4},{5,7},{7,5},{8,10},{10,8},{9,1... | collective-permute-start | bytes 12296 | tf_op jit(solution)/shard_map/ppermute | solution.py:516
  30.8 1.6 %field.5.refs_6_ = f32[64,128,128]{2,1,0:T(8,128)} custom-call(f32[2160,128]{1,0:T(8,128)S(1)} %get-tuple-element.17.refs_0_, f32[8,128]{1,0:T(8,128)S(1)} %get-tuple-element.13.refs_1_, bf16[128,176]{1,0:T(8,128)(2,1)S(1)} %get-tuple-element.18.refs_2_, bf16[4,256,128]{2,1,0:T(8,128)(2,1)S(1)} %get-tuple-element.19.refs_3_, ...), custom_call_target="tpu_custom_call", output_to_operand_aliasing={{}: (6, {})} | custom-call | flops 1000000000 | bytes 1048576 | tf_op jit(solution)/shard_map/field/pallas_call | solution.py:523
  32.4 1.4 %collective-permute-done.5 = f32[8,128]{1,0:T(8,128)S(1)} collective-permute-done((f32[8,128]{1,0:T(8,128)S(1)}, f32[8,128]{1,0:T(8,128)S(1)}, u32[]{:S(2)}, u32[]{:S(2)}) %collective-permute-start.5) | collective-permute-done | bytes 4128 | tf_op jit(solution)/shard_map/ppermute | solution.py:516
  33.9 1.6 %collective-permute-start.6 = (f32[8,128]{1,0:T(8,128)S(1)}, f32[8,128]{1,0:T(8,128)S(1)}, u32[]{:S(2)}, u32[]{:S(2)}) collective-permute-start(f32[8,128]{1,0:T(8,128)S(1)} %add.13.refs_5_), channel_id=1, source_target_pairs={{0,4},{4,0},{8,12},{12,8},{1,5},{5,1},{9,13},{13,9},{2,6},{6,2},{1... | collective-permute-start | bytes 12296 | tf_op jit(solution)/shard_map/ppermute | solution.py:516
  35.5 1.6 %field.6.refs_6_ = f32[64,128,128]{2,1,0:T(8,128)} custom-call(f32[2160,128]{1,0:T(8,128)S(1)} %get-tuple-element.17.refs_0_, f32[8,128]{1,0:T(8,128)S(1)} %get-tuple-element.13.refs_1_, bf16[128,176]{1,0:T(8,128)(2,1)S(1)} %get-tuple-element.18.refs_2_, bf16[4,256,128]{2,1,0:T(8,128)(2,1)S(1)} %get-tuple-element.19.refs_3_, ...), custom_call_target="tpu_custom_call", output_to_operand_aliasing={{}: (6, {})} | custom-call | flops 1000000000 | bytes 1048576 | tf_op jit(solution)/shard_map/field/pallas_call | solution.py:523
  37.1 0.4 collective-permute-done.6
  37.5 2.6 %collective-permute-start.7 = (f32[8,128]{1,0:T(8,128)S(1)}, f32[8,128]{1,0:T(8,128)S(1)}, u32[]{:S(2)}, u32[]{:S(2)}) collective-permute-start(f32[8,128]{1,0:T(8,128)S(1)} %add.14.refs_5_), channel_id=1, source_target_pairs={{0,8},{4,12},{8,0},{12,4},{1,9},{5,13},{9,1},{13,5},{2,10},{6,14},... | collective-permute-start | bytes 12296 | tf_op jit(solution)/shard_map/ppermute | solution.py:516
  40.1 1.6 %field.7 = f32[64,128,128]{2,1,0:T(8,128)} custom-call(f32[2160,128]{1,0:T(8,128)S(1)} %get-tuple-element.17.refs_0_, f32[8,128]{1,0:T(8,128)S(1)} %get-tuple-element.13.refs_1_, bf16[128,176]{1,0:T(8,128)(2,1)S(1)} %get-tuple-element.18.refs_2_, bf16[4,256,128]{2,1,0:T(8,128)(2,1)S(1)} %get-tuple-element.19.refs_3_, ...), custom_call_target="tpu_custom_call", output_to_operand_aliasing={{}: (6, {})} | custom-call | flops 1000000000 | bytes 1048576 | tf_op jit(solution)/shard_map/field/pallas_call | solution.py:523
  41.7 0.3 collective-permute-done.7
  42.0 0.6 %add_reduce_fusion = f32[]{:T(128)} fusion(f32[8,128]{1,0:T(8,128)S(1)} %add.14.refs_5_, f32[8,128]{1,0:T(8,128)S(1)} %collective-permute-done.7), kind=kLoop, calls=%fused_computation.4 | loop fusion | flops 2047 | bytes 8196 | tf_op jit(solution)/shard_map/reduce_sum | solution.py:541
  (7 shorter events, 0.0 us)
Async XLA Ops:
  1.3 0.7 %copy-start = (f32[3,256]{1,0:T(4,128)S(1)}, f32[3,256]{1,0:T(4,128)}, u32[]{:S(2)}) copy-start(f32[3,256]{1,0:T(4,128)} %offsets.1) | copy-start | bytes 9220
  2.0 0.7 %copy-start.1 = (s32[256]{0:T(256)S(1)}, s32[256]{0:T(256)}, u32[]{:S(2)}) copy-start(s32[256]{0:T(256)} %param.8) | copy-start | bytes 3076
  2.6 0.7 %copy-start.2 = (s32[256]{0:T(256)S(1)}, s32[256]{0:T(256)}, u32[]{:S(2)}) copy-start(s32[256]{0:T(256)} %param.9) | copy-start | bytes 3076
  3.3 0.7 %copy-start.3 = (s32[256]{0:T(256)S(1)}, s32[256]{0:T(256)}, u32[]{:S(2)}) copy-start(s32[256]{0:T(256)} %param.10) | copy-start | bytes 3076
  4.0 0.7 %copy-start.4 = (f32[256]{0:T(256)S(1)}, f32[256]{0:T(256)}, u32[]{:S(2)}) copy-start(f32[256]{0:T(256)} %param.12) | copy-start | bytes 3076
  4.7 0.7 %copy-start.5 = (f32[4]{0:T(128)S(1)}, f32[4]{0:T(128)}, u32[]{:S(2)}) copy-start(f32[4]{0:T(128)} %amplitude.1) | copy-start | bytes 52
  6.0 1.4 %collective-permute-start = (f32[1,4,256]{2,1,0:T(4,128)S(1)}, f32[1,4,256]{2,1,0:T(4,128)S(1)}, u32[]{:S(2)}, u32[]{:S(2)}) collective-permute-start(f32[1,4,256]{2,1,0:T(4,128)S(1)} %get-tuple-element.12), channel_id=1, source_target_pairs={{0,1},{1,0},{2,3},{3,2},{4,5},{5,4},{6,7},{7,6},{8,9},{9,8},{10,11... | collective-permute-start | bytes 12296 | tf_op jit(solution)/shard_map/ppermute | solution.py:487
  7.4 8.8 %collective-permute-start.1 = (f32[2,4,256]{2,1,0:T(4,128)S(1)}, f32[2,4,256]{2,1,0:T(4,128)S(1)}, u32[]{:S(2)}, u32[]{:S(2)}) collective-permute-start(f32[2,4,256]{2,1,0:T(4,128)S(1)} %constant_dynamic-update-slice_fusion.refs_1_.refs_5_), channel_id=1, source_target_pairs={{0,2},{2,0},{1,3},{3,1},{4,6},{6,4},{5,7},{7,5},{8,10},{10,8},{9,1... | collective-permute-start | bytes 24584 | tf_op jit(solution)/shard_map/ppermute | solution.py:487
  10.2 2.2 %copy-start.6 = (f32[64,128,128]{2,1,0:T(8,128)S(1)}, f32[64,128,128]{2,1,0:T(8,128)}, u32[]{:S(2)}) copy-start(f32[64,128,128]{2,1,0:T(8,128)} %refs_0_.1) | copy-start | bytes 12582916
  16.3 3.8 %collective-permute-start.2 = (f32[4,4,256]{2,1,0:T(4,128)S(1)}, f32[4,4,256]{2,1,0:T(4,128)S(1)}, u32[]{:S(2)}, u32[]{:S(2)}) collective-permute-start(f32[4,4,256]{2,1,0:T(4,128)S(1)} %pad_maximum_fusion.1), channel_id=1, source_target_pairs={{0,4},{4,0},{8,12},{12,8},{1,5},{5,1},{9,13},{13,9},{2,6},{6,2},{1... | collective-permute-start | bytes 49160 | tf_op jit(solution)/shard_map/ppermute | solution.py:487
  20.1 4.9 %collective-permute-start.3 = (f32[8,4,256]{2,1,0:T(4,128)S(1)}, f32[8,4,256]{2,1,0:T(4,128)S(1)}, u32[]{:S(2)}, u32[]{:S(2)}) collective-permute-start(f32[8,4,256]{2,1,0:T(4,128)S(1)} %pad_maximum_fusion), channel_id=1, source_target_pairs={{0,8},{4,12},{8,0},{12,4},{1,9},{5,13},{9,1},{13,5},{2,10},{6,14},... | collective-permute-start | bytes 98312 | tf_op jit(solution)/shard_map/ppermute | solution.py:487
  28.5 1.7 %collective-permute-start.4 = (f32[8,128]{1,0:T(8,128)S(1)}, f32[8,128]{1,0:T(8,128)S(1)}, u32[]{:S(2)}, u32[]{:S(2)}) collective-permute-start(f32[8,128]{1,0:T(8,128)S(1)} %get-tuple-element.21.refs_5_), channel_id=1, source_target_pairs={{0,1},{1,0},{2,3},{3,2},{4,5},{5,4},{6,7},{7,6},{8,9},{9,8},{10,11... | collective-permute-start | bytes 12296 | tf_op jit(solution)/shard_map/ppermute | solution.py:516
  30.3 3.6 %collective-permute-start.5 = (f32[8,128]{1,0:T(8,128)S(1)}, f32[8,128]{1,0:T(8,128)S(1)}, u32[]{:S(2)}, u32[]{:S(2)}) collective-permute-start(f32[8,128]{1,0:T(8,128)S(1)} %add.12.refs_5_), channel_id=1, source_target_pairs={{0,2},{2,0},{1,3},{3,1},{4,6},{6,4},{5,7},{7,5},{8,10},{10,8},{9,1... | collective-permute-start | bytes 12296 | tf_op jit(solution)/shard_map/ppermute | solution.py:516
  33.9 3.6 %collective-permute-start.6 = (f32[8,128]{1,0:T(8,128)S(1)}, f32[8,128]{1,0:T(8,128)S(1)}, u32[]{:S(2)}, u32[]{:S(2)}) collective-permute-start(f32[8,128]{1,0:T(8,128)S(1)} %add.13.refs_5_), channel_id=1, source_target_pairs={{0,4},{4,0},{8,12},{12,8},{1,5},{5,1},{9,13},{13,9},{2,6},{6,2},{1... | collective-permute-start | bytes 12296 | tf_op jit(solution)/shard_map/ppermute | solution.py:516
  37.5 4.5 %collective-permute-start.7 = (f32[8,128]{1,0:T(8,128)S(1)}, f32[8,128]{1,0:T(8,128)S(1)}, u32[]{:S(2)}, u32[]{:S(2)}) collective-permute-start(f32[8,128]{1,0:T(8,128)S(1)} %add.14.refs_5_), channel_id=1, source_target_pairs={{0,8},{4,12},{8,0},{12,4},{1,9},{5,13},{9,1},{13,5},{2,10},{6,14},... | collective-permute-start | bytes 12296 | tf_op jit(solution)/shard_map/ppermute | solution.py:516
where the time goes:
time: 44.7 us; the launch traced here: 44.4 us
  Pallas kernels  19.2 us (43%)
  starting transfers between devices  12.3 us (28%)
  local copies, waits for them, and re-layouts  6.25 us (14%)
  between operations  3.17 us (7%)
  waiting for transfers between devices  2.73 us (6%)
  other arithmetic  0.7 us (2%)
    pallas_call x4, Pallas kernels, spread(): pl.pallas_call(lambda *refs: spread_kernel(plan, together, first, last, *...  8.72 us
    ppermute x4, starting transfers between devices, on_device(): got = lax.ppermute(held, axis, pairs)  7.53 us
    pallas_call x4, Pallas kernels, on_device(): pl.pallas_call(lambda *refs, part=number: field_kernel(plan, part, parts,...  6.55 us
    unnamed x15, local copies, waits for them, and re-layouts  6.24 us
    ppermute x4, starting transfers between devices, on_device(): got = lax.ppermute(energy, axis, pairs)  4.77 us
    pallas_call x1, Pallas kernels, on_device(): pl.pallas_call(lambda *refs: turned_kernel(plan, *refs), out_shape=grid_s...  2.5 us
    ppermute x4, waiting for transfers between devices, on_device(): got = lax.ppermute(energy, axis, pairs)  2.11 us
  transfers between devices with their start and end apart: 8, of which 4 were waited for; matrix products, arithmetic and copies ran while one was open for 0% of the time, Pallas kernels for 34%

commit v1 on v0

--- a/solution.py
+++ b/solution.py
@@ -151,40 +151,27 @@
     hat_x_turned[...] = edge_hat(plan, hat_x_turned.shape, 1).astype(jnp.bfloat16)
 
 
-def prepare_kernel(
-    cell_x, cell_y, cell_z, offsets, charge, counts, amplitude, mine, scales,
-    cells, shifts, held, levels, live, sems,
-):
+def prepare_kernel(packed, mine, consts):
     blocks = mine.shape[0]
-    copies = [
-        pltpu.make_async_copy(source, target, sems.at[number])
-        for number, (source, target) in enumerate(
-            [
-                (cell_x, cells.at[0]),
-                (cell_y, cells.at[1]),
-                (cell_z, cells.at[2]),
-                (offsets, shifts),
-                (charge, held),
-                (counts, live),
-                (amplitude, levels),
-            ]
-        )
-    ]
-    for copy in copies:
-        copy.start()
-    for copy in copies:
-        copy.wait()
-    slot = lax.broadcasted_iota(jnp.int32, (1, BQ), 1)
+    slot = lax.broadcasted_iota(jnp.int32, (1, BQ), 1).astype(jnp.float32)
     for block in range(blocks):
         columns = slice(block * BQ, (block + 1) * BQ)
-        mine[block, 0:1] = jnp.where(slot < live[block], held[:, columns], 0.0)
-        for axis in range(3):
-            mine[block, axis + 1 : axis + 2] = (
-                cells[axis, :, columns].astype(jnp.float32) + shifts[axis : axis + 1, columns]
-            )
+        live = packed[5:6, block : block + 1]
+        mine[block, 0:1] = jnp.where(slot < live, packed[0:1, columns], 0.0)
+        mine[block, 1:4] = packed[1:4, columns]
+    shape = (1, consts.shape[1])
     for level in range(LEVELS):
-        scales[level : level + 1] = jnp.full((1, scales.shape[1]), levels[level], jnp.float32)
-    scales[LEVELS:] = jnp.zeros((8 - LEVELS, scales.shape[1]), jnp.float32)
+        consts[level : level + 1] = jnp.broadcast_to(packed[4:5, level : level + 1], shape)
+    for axis in range(3):
+        consts[LEVELS + axis : LEVELS + axis + 1] = jnp.broadcast_to(
+            packed[6:7, axis : axis + 1], shape
+        )
+    consts[LEVELS + 3 :] = jnp.zeros(shape, jnp.float32)
+
+
+def finish_kernel(scale, energy, got, out):
+    total = jnp.sum(energy[...] + got[...], axis=0, keepdims=True)
+    out[...] = jnp.sum(total, axis=1, keepdims=True) * scale
 
 
 def weights(position, first, dim, base, rows):
@@ -197,14 +184,14 @@
 
 def spread_kernel(plan, together, first, last, *refs):
     refs = list(refs)
-    starts, charges = refs[:2]
+    consts, charges = refs[:2]
     before = None if first else refs[2]
     turned = refs[2 if first else 3] if last else None
     outs = refs[2 + (not first) + last :]
     if last:
         energy = outs.pop(1)
     grids, along_x, along_y, along_z, planes = outs
-    begin = [starts[axis].astype(jnp.float32) for axis in range(3)]
+    begin = [consts[LEVELS + axis : LEVELS + axis + 1, :1] for axis in range(3)]
     steps = charges.shape[0] // together
 
     def one_step(step, before):
@@ -423,35 +410,39 @@
     hat_y, hat_y_turned, hat_z, hat_z_turned, hat_x, hat_x_turned = hats
 
     slots = blocks * BQ
-    mine, scales = pl.pallas_call(
+    row = lax.broadcasted_iota(jnp.int32, (8, slots), 0)
+    column = lax.broadcasted_iota(jnp.int32, (8, slots), 1)
+
+    def wide(vector):
+        return jnp.pad(vector.astype(f32), (0, slots - vector.shape[0]))[None, :]
+
+    index = [lax.axis_index(axis).astype(f32) for axis in axes]
+    index = jnp.where(column == 0, index[0], jnp.where(column == 1, index[1], index[2]))
+    places = jnp.where(row == 1, cell_x[None], jnp.where(row == 2, cell_y[None], cell_z[None]))
+    places = places.astype(f32) + jnp.pad(offsets, ((1, 4), (0, 0)))
+    packed = jnp.where(
+        row == 0,
+        charge[None],
+        jnp.where(
+            row < 4,
+            places,
+            jnp.where(
+                row == 4, wide(level_amplitude), jnp.where(row == 5, wide(block_count), index)
+            ),
+        ),
+    )
+    mine, consts = pl.pallas_call(
         prepare_kernel,
         out_shape=[
             jax.ShapeDtypeStruct((blocks, 4, BQ), f32),
             jax.ShapeDtypeStruct((8, 128), f32),
         ],
-        in_specs=[hbm] * 7,
+        in_specs=[vmem],
         out_specs=[vmem] * 2,
-        scratch_shapes=[
-            pltpu.VMEM((3, 1, slots), jnp.int32),
-            pltpu.VMEM((3, slots), f32),
-            pltpu.VMEM((1, slots), f32),
-            pltpu.SMEM((LEVELS,), f32),
-            pltpu.SMEM((blocks,), jnp.int32),
-            pltpu.SemaphoreType.DMA((7,)),
-        ],
         compiler_params=params,
         name="prepare",
-    )(
-        cell_x.reshape(1, slots),
-        cell_y.reshape(1, slots),
-        cell_z.reshape(1, slots),
-        offsets,
-        charge.reshape(1, slots),
-        block_count,
-        level_amplitude,
-    )
-
-    starts = jnp.stack([lax.axis_index(axis) for axis in axes]).astype(jnp.int32)
+    )(packed)
+
     grid_shape = jax.ShapeDtypeStruct((plan.total, plan.width), f32)
 
     def spread(charges, before, turned):
@@ -459,11 +450,11 @@
         together = math.gcd(count, 4)
         deep = together * BQ
         first, last = before is None, turned is not None
-        operands = [starts, charges] + [x for x in (before, turned) if x is not None]
+        operands = [consts, charges] + [x for x in (before, turned) if x is not None]
         return pl.pallas_call(
             lambda *refs: spread_kernel(plan, together, first, last, *refs),
             out_shape=[grid_shape] + [jax.ShapeDtypeStruct((8, plan.width), f32)] * last,
-            in_specs=[smem] + [vmem] * (len(operands) - 1),
+            in_specs=[vmem] * len(operands),
             out_specs=[vmem] * (1 + last),
             scratch_shapes=[
                 pltpu.VMEM((plan.off_x[-1], BQ), f32),
@@ -501,9 +492,9 @@
                 cost_estimate=pl.CostEstimate(
                     flops=2 * 10**9, bytes_accessed=math.prod(rows) * 4, transcendentals=0
                 ),
-                compiler_params=params,
+                compiler_params=pltpu.CompilerParams(vmem_limit_bytes=51 * 2**20),
                 name="turned",
-            )(density, scales, hat_y_turned, hat_z_turned, hat_x_turned, held)
+            )(density, consts, hat_y_turned, hat_z_turned, hat_x_turned, held)
         new = held if number == 0 else got
         end = number == len(steps) - 1
         out = spread(new, grids, turned if end else None)
@@ -515,7 +506,7 @@
     for number, (axis, pairs) in enumerate(steps):
         got = lax.ppermute(energy, axis, pairs)
         if number < parts:
-            operands = [grids, scales, hat_y, hat_z, hat_x, energy]
+            operands = [grids, consts, hat_y, hat_z, hat_x, energy]
             specs = [vmem] * len(operands)
             if field is not None:
                 operands.append(field)
@@ -536,10 +527,18 @@
                 compiler_params=params,
                 name="field",
             )(*operands)
-        energy = energy + got
+        if number < len(steps) - 1:
+            energy = energy + got
     fine = math.prod(count * lax.axis_size(axis) for count, axis in zip(rows, axes))
-    energy = jnp.sum(energy.reshape(1, -1), axis=1) / fine
-    return field, energy
+    energy = pl.pallas_call(
+        lambda *refs: finish_kernel(1.0 / fine, *refs),
+        out_shape=jax.ShapeDtypeStruct((1, 1), f32),
+        in_specs=[vmem] * 2,
+        out_specs=vmem,
+        compiler_params=params,
+        name="finish",
+    )(energy, got)
+    return field, energy.reshape(1)
 
 
 def solution(mesh):

time: 44.7 us -> 37.7 us (0.84)
  local copies, waits for them, and re-layouts: 6.25 us -> 0.68 us
  between operations: 3.17 us -> 1.4 us
  waiting for transfers between devices: 2.73 us -> 3.9 us
  Pallas kernels: 19.2 us -> 18.7 us
    unnamed x15 -> x1, local copies, waits for them, and re-layouts: 6.24 us -> 0.01 us
    pallas_call x4, Pallas kernels: 8.72 us -> 7.2 us  [spread(): pl.pallas_call(lambda *refs: spread_kernel(plan, together, first, last, *...]
    pallas_call x1, Pallas kernels: 2.5 us -> 3.44 us  [on_device(): pl.pallas_call(lambda *refs: turned_kernel(plan, *refs), out_shape=grid_s...]
    ppermute x4, waiting for transfers between devices: 0.62 us -> 1.48 us  [on_device(): got = lax.ppermute(held, axis, pairs)]
    select_n x0 -> x2, other arithmetic: none -> 0.82 us  [the longest x1 0.82 us: on_device(): jnp.where(row == 0, charge[None], jnp.where(row < 4, places, jnp.where(ro...]
    pad x0 -> x2, local copies, waits for them, and re-layouts: none -> 0.67 us  [wide(): return jnp.pad(vector.astype(f32), (0, slots - vector.shape[0]))[None, :]]
    reduce_sum x1 -> x0, other arithmetic: 0.6 us -> none  [on_device(): energy = jnp.sum(energy.reshape(1, -1), axis=1) / fine]
    pallas_call x0 -> x1, Pallas kernels: none -> 0.59 us  [on_device(): pl.pallas_call(lambda *refs: finish_kernel(1.0 / fine, *refs), out_shape=...]
  transfers between devices with their start and end apart: 8 -> 8, of which waited for: 4 -> 5; matrix products, arithmetic and copies ran while one was open for 0% -> 0% of each run, Pallas kernels for 34% -> 39%
where the time goes in v1:
time: 37.7 us; the launch traced here: 37.6 us
  Pallas kernels  18.7 us (50%)
  starting transfers between devices  12 us (32%)
  waiting for transfers between devices  3.9 us (10%)
  between operations  1.4 us (4%)
  other arithmetic  0.87 us (2%)
  local copies, waits for them, and re-layouts  0.68 us (2%)
    ppermute x4, starting transfers between devices, on_device(): got = lax.ppermute(held, axis, pairs)  7.55 us
    pallas_call x4, Pallas kernels, spread(): pl.pallas_call(lambda *refs: spread_kernel(plan, together, first, last, *...  7.2 us
    pallas_call x4, Pallas kernels, on_device(): pl.pallas_call(lambda *refs, part=number: field_kernel(plan, part, parts,...  6.54 us
    ppermute x4, starting transfers between devices, on_device(): got = lax.ppermute(energy, axis, pairs)  4.47 us
    pallas_call x1, Pallas kernels, on_device(): pl.pallas_call(lambda *refs: turned_kernel(plan, *refs), out_shape=grid_s...  3.44 us
    ppermute x4, waiting for transfers between devices, on_device(): got = lax.ppermute(energy, axis, pairs)  2.42 us
    ppermute x4, waiting for transfers between devices, on_device(): got = lax.ppermute(held, axis, pairs)  1.48 us
    pallas_call x1, Pallas kernels, on_device(): pl.pallas_call(lambda *refs: hats_kernel(plan, *refs), out_shape=[jax.Sha...  0.84 us
  transfers between devices with their start and end apart: 8, of which 5 were waited for; matrix products, arithmetic and copies ran while one was open for 0% of the time, Pallas kernels for 39%

profile of v1, /device:TPU:0, one launch (start us, length us, event | category | flops | bytes accessed | tf_op | source)
XLA Modules:
  0.0 37.6 jit_solution(11959968730071556144)
XLA Ops:
  1.3 0.7 %pad.13 = f32[256]{0:T(256)S(1)} pad(f32[4]{0:T(128)} %param.14, f32[]{:T(128)} %constant.19.clone.1), padding=0_252 | pad | bytes 1044 | tf_op jit(solution)/shard_map/jit(_pad)/pad | solution.py:417
  2.0 0.8 %select_select_fusion.packed = f32[8,256]{1,0:T(8,128)S(1)} fusion(f32[3,256]{1,0:T(4,128)} %param.11, f32[256]{0:T(256)S(1)} %compare_select_fusion, f32[]{:T(128)S(6)} %convert_element_type.23, f32[256]{0:T(256)S(1)} %pad.14, f32[256]{0:T(256)S(1)} %pad.13, s32[256]{0:T(256)} %param.10, s32[256]{0:T(256)} %param.9, s32[256]{0:T(256)} %param.8, ...), kind=kLoop, calls=%fused_computation.2 | loop fusion | flops 18432 | bytes 18740 | tf_op jit(solution)/shard_map/jit(_where)/select_n | solution.py:423
  2.8 0.1 prepare.1
  2.9 0.5 %collective-permute-start = (f32[1,4,256]{2,1,0:T(4,128)S(1)}, f32[1,4,256]{2,1,0:T(4,128)S(1)}, u32[]{:S(2)}, u32[]{:S(2)}) collective-permute-start(f32[1,4,256]{2,1,0:T(4,128)S(1)} %get-tuple-element.13), channel_id=1, source_target_pairs={{0,1},{1,0},{2,3},{3,2},{4,5},{5,4},{6,7},{7,6},{8,9},{9,8},{10,11... | collective-permute-start | bytes 12296 | tf_op jit(solution)/shard_map/ppermute | solution.py:478
  3.4 0.8 %hats.1 = (bf16[128,176]{1,0:T(8,128)(2,1)S(1)}, bf16[176,256]{1,0:T(8,128)(2,1)S(1)}, bf16[4,256,128]{2,1,0:T(8,128)(2,1)S(1)}, bf16[4,256,128]{2,1,0:T(8,128)(...) custom-call(), custom_call_target="tpu_custom_call" | custom-call | tf_op jit(solution)/shard_map/hats/pallas_call | solution.py:393
  4.2 0.0 collective-permute-done
  4.2 2.8 %collective-permute-start.1 = (f32[2,4,256]{2,1,0:T(4,128)S(1)}, f32[2,4,256]{2,1,0:T(4,128)S(1)}, u32[]{:S(2)}, u32[]{:S(2)}) collective-permute-start(f32[2,4,256]{2,1,0:T(4,128)S(1)} %constant_dynamic-update-slice_fusion.refs_1_.refs_5_), channel_id=1, source_target_pairs={{0,2},{2,0},{1,3},{3,1},{4,6},{6,4},{5,7},{7,5},{8,10},{10,8},{9,1... | collective-permute-start | bytes 24584 | tf_op jit(solution)/shard_map/ppermute | solution.py:478
  7.0 3.4 %turned.1.refs_3_ = f32[2160,128]{1,0:T(8,128)S(1)} custom-call(f32[64,128,128]{2,1,0:T(8,128)} %refs_0_.1, f32[8,128]{1,0:T(8,128)S(1)} %get-tuple-element.12.refs_0_.refs_1_, bf16[176,256]{1,0:T(8,128)(2,1)S(1)} %get-tuple-element.14.refs_2_, bf16[4,256,128]{2,1,0:T(8,128)(2,1)S(1)} %get-tuple-element.15.refs_3_, ...), custom_call_target="tpu_custom_call" | custom-call | flops 2000000000 | bytes 4194304 | tf_op jit(solution)/shard_map/turned/pallas_call | solution.py:481
  10.5 1.0 %spread.4.refs_2_ = f32[2160,128]{1,0:T(8,128)S(1)} custom-call(f32[8,128]{1,0:T(8,128)S(1)} %get-tuple-element.12.refs_0_.refs_1_, f32[2,4,256]{2,1,0:T(4,128)S(1)} %constant_dynamic-update-slice_fusion.refs_1_.refs_5_), custom_call_target="tpu_custom_call" | custom-call | flops 566231040 | tf_op jit(solution)/shard_map/spread/pallas_call | solution.py:454
  11.5 0.0 collective-permute-done.1.refs_1_
  11.5 1.6 %collective-permute-start.2 = (f32[4,4,256]{2,1,0:T(4,128)S(1)}, f32[4,4,256]{2,1,0:T(4,128)S(1)}, u32[]{:S(2)}, u32[]{:S(2)}) collective-permute-start(f32[4,4,256]{2,1,0:T(4,128)S(1)} %pad_maximum_fusion.1), channel_id=1, source_target_pairs={{0,4},{4,0},{8,12},{12,8},{1,5},{5,1},{9,13},{13,9},{2,6},{6,2},{1... | collective-permute-start | bytes 49160 | tf_op jit(solution)/shard_map/ppermute | solution.py:478
  13.1 1.1 %spread.5.refs_2_ = f32[2160,128]{1,0:T(8,128)S(1)} custom-call(f32[8,128]{1,0:T(8,128)S(1)} %get-tuple-element.12.refs_0_.refs_1_, f32[2,4,256]{2,1,0:T(4,128)S(1)} %collective-permute-done.1.refs_1_, f32[2160,128]{1,0:T(8,128)S(1)} %spread.4.refs_2_), custom_call_target="tpu_custom_call", output_to_operand_aliasing={{}: (2, {})} | custom-call | flops 566231040 | tf_op jit(solution)/shard_map/spread/pallas_call | solution.py:454
  14.2 1.1 %collective-permute-done.2.refs_1_ = f32[4,4,256]{2,1,0:T(4,128)S(1)} collective-permute-done((f32[4,4,256]{2,1,0:T(4,128)S(1)}, f32[4,4,256]{2,1,0:T(4,128)S(1)}, u32[]{:S(2)}, u32[]{:S(2)}) %collective-permute-start.2) | collective-permute-done | bytes 16416 | tf_op jit(solution)/shard_map/ppermute | solution.py:478
  15.3 2.7 %collective-permute-start.3 = (f32[8,4,256]{2,1,0:T(4,128)S(1)}, f32[8,4,256]{2,1,0:T(4,128)S(1)}, u32[]{:S(2)}, u32[]{:S(2)}) collective-permute-start(f32[8,4,256]{2,1,0:T(4,128)S(1)} %pad_maximum_fusion), channel_id=1, source_target_pairs={{0,8},{4,12},{8,0},{12,4},{1,9},{5,13},{9,1},{13,5},{2,10},{6,14},... | collective-permute-start | bytes 98312 | tf_op jit(solution)/shard_map/ppermute | solution.py:478
  18.0 1.8 %spread.6.refs_2_ = f32[2160,128]{1,0:T(8,128)S(1)} custom-call(f32[8,128]{1,0:T(8,128)S(1)} %get-tuple-element.12.refs_0_.refs_1_, f32[4,4,256]{2,1,0:T(4,128)S(1)} %collective-permute-done.2.refs_1_, f32[2160,128]{1,0:T(8,128)S(1)} %spread.5.refs_2_), custom_call_target="tpu_custom_call", output_to_operand_aliasing={{}: (2, {})} | custom-call | flops 1132462080 | tf_op jit(solution)/shard_map/spread/pallas_call | solution.py:454
  19.8 0.4 %collective-permute-done.3.refs_1_ = f32[8,4,256]{2,1,0:T(4,128)S(1)} collective-permute-done((f32[8,4,256]{2,1,0:T(4,128)S(1)}, f32[8,4,256]{2,1,0:T(4,128)S(1)}, u32[]{:S(2)}, u32[]{:S(2)}) %collective-permute-start.3) | collective-permute-done | bytes 32800 | tf_op jit(solution)/shard_map/ppermute | solution.py:478
  20.2 3.3 %spread.7 = (f32[2160,128]{1,0:T(8,128)S(1)}, f32[8,128]{1,0:T(8,128)S(1)}) custom-call(f32[8,128]{1,0:T(8,128)S(1)} %get-tuple-element.12.refs_0_.refs_1_, f32[8,4,256]{2,1,0:T(4,128)S(1)} %collective-permute-done.3.refs_1_, f32[2160,128]{1,0:T(8,128)S(1)} %spread.6.refs_2_, f32[2160,128]{1,0:T(8,128)S(1)} %turned.1.refs_3_), custom_call_target="tpu_custom_call", output_to_operand_aliasing={{0}: (2, {})} | custom-call | flops 2264924160 | tf_op jit(solution)/shard_map/spread/pallas_call | solution.py:454
  23.5 0.1 collective-permute-start.4
  23.6 1.6 %field.4.refs_6_ = f32[64,128,128]{2,1,0:T(8,128)} custom-call(f32[2160,128]{1,0:T(8,128)S(1)} %get-tuple-element.17.refs_0_, f32[8,128]{1,0:T(8,128)S(1)} %get-tuple-element.12.refs_0_.refs_1_, bf16[128,176]{1,0:T(8,128)(2,1)S(1)} %get-tuple-element.18.refs_2_, bf16[4,256,128]{2,1,0:T(8,128)(2,1)S(1)} %get-tuple-element.19.refs_3_, ...), custom_call_target="tpu_custom_call" | custom-call | flops 1000000000 | bytes 1048576 | tf_op jit(solution)/shard_map/field/pallas_call | solution.py:514
  25.2 0.0 collective-permute-done.4
  25.2 0.2 collective-permute-start.5
  25.4 1.6 %field.5.refs_6_ = f32[64,128,128]{2,1,0:T(8,128)} custom-call(f32[2160,128]{1,0:T(8,128)S(1)} %get-tuple-element.17.refs_0_, f32[8,128]{1,0:T(8,128)S(1)} %get-tuple-element.12.refs_0_.refs_1_, bf16[128,176]{1,0:T(8,128)(2,1)S(1)} %get-tuple-element.18.refs_2_, bf16[4,256,128]{2,1,0:T(8,128)(2,1)S(1)} %get-tuple-element.19.refs_3_, ...), custom_call_target="tpu_custom_call", output_to_operand_aliasing={{}: (6, {})} | custom-call | flops 1000000000 | bytes 1048576 | tf_op jit(solution)/shard_map/field/pallas_call | solution.py:514
  27.1 1.8 %collective-permute-done.5 = f32[8,128]{1,0:T(8,128)S(1)} collective-permute-done((f32[8,128]{1,0:T(8,128)S(1)}, f32[8,128]{1,0:T(8,128)S(1)}, u32[]{:S(2)}, u32[]{:S(2)}) %collective-permute-start.5) | collective-permute-done | bytes 4128 | tf_op jit(solution)/shard_map/ppermute | solution.py:507
  28.8 1.6 %collective-permute-start.6 = (f32[8,128]{1,0:T(8,128)S(1)}, f32[8,128]{1,0:T(8,128)S(1)}, u32[]{:S(2)}, u32[]{:S(2)}) collective-permute-start(f32[8,128]{1,0:T(8,128)S(1)} %add.20.refs_5_), channel_id=1, source_target_pairs={{0,4},{4,0},{8,12},{12,8},{1,5},{5,1},{9,13},{13,9},{2,6},{6,2},{1... | collective-permute-start | bytes 12296 | tf_op jit(solution)/shard_map/ppermute | solution.py:507
  30.4 1.6 %field.6.refs_6_ = f32[64,128,128]{2,1,0:T(8,128)} custom-call(f32[2160,128]{1,0:T(8,128)S(1)} %get-tuple-element.17.refs_0_, f32[8,128]{1,0:T(8,128)S(1)} %get-tuple-element.12.refs_0_.refs_1_, bf16[128,176]{1,0:T(8,128)(2,1)S(1)} %get-tuple-element.18.refs_2_, bf16[4,256,128]{2,1,0:T(8,128)(2,1)S(1)} %get-tuple-element.19.refs_3_, ...), custom_call_target="tpu_custom_call", output_to_operand_aliasing={{}: (6, {})} | custom-call | flops 1000000000 | bytes 1048576 | tf_op jit(solution)/shard_map/field/pallas_call | solution.py:514
  32.1 0.4 %collective-permute-done.6 = f32[8,128]{1,0:T(8,128)S(1)} collective-permute-done((f32[8,128]{1,0:T(8,128)S(1)}, f32[8,128]{1,0:T(8,128)S(1)}, u32[]{:S(2)}, u32[]{:S(2)}) %collective-permute-start.6) | collective-permute-done | bytes 4128 | tf_op jit(solution)/shard_map/ppermute | solution.py:507
  32.5 2.6 %collective-permute-start.7 = (f32[8,128]{1,0:T(8,128)S(1)}, f32[8,128]{1,0:T(8,128)S(1)}, u32[]{:S(2)}, u32[]{:S(2)}) collective-permute-start(f32[8,128]{1,0:T(8,128)S(1)} %add.21.refs_5_.refs_0_), channel_id=1, source_target_pairs={{0,8},{4,12},{8,0},{12,4},{1,9},{5,13},{9,1},{13,5},{2,10},{6,14},... | collective-permute-start | bytes 12296 | tf_op jit(solution)/shard_map/ppermute | solution.py:507
  35.1 1.6 %field.7 = f32[64,128,128]{2,1,0:T(8,128)} custom-call(f32[2160,128]{1,0:T(8,128)S(1)} %get-tuple-element.17.refs_0_, f32[8,128]{1,0:T(8,128)S(1)} %get-tuple-element.12.refs_0_.refs_1_, bf16[128,176]{1,0:T(8,128)(2,1)S(1)} %get-tuple-element.18.refs_2_, bf16[4,256,128]{2,1,0:T(8,128)(2,1)S(1)} %get-tuple-element.19.refs_3_, ...), custom_call_target="tpu_custom_call", output_to_operand_aliasing={{}: (6, {})} | custom-call | flops 1000000000 | bytes 1048576 | tf_op jit(solution)/shard_map/field/pallas_call | solution.py:514
  36.7 0.3 collective-permute-done.7.refs_1_
  37.0 0.6 %finish.1 = f32[1,1]{1,0:T(1,128)} custom-call(f32[8,128]{1,0:T(8,128)S(1)} %add.21.refs_5_.refs_0_, f32[8,128]{1,0:T(8,128)S(1)} %collective-permute-done.7.refs_1_), custom_call_target="tpu_custom_call" | custom-call | tf_op jit(solution)/shard_map/finish/pallas_call | solution.py:533
  (13 shorter events, 0.1 us)
Async XLA Ops:
  2.9 1.3 %collective-permute-start = (f32[1,4,256]{2,1,0:T(4,128)S(1)}, f32[1,4,256]{2,1,0:T(4,128)S(1)}, u32[]{:S(2)}, u32[]{:S(2)}) collective-permute-start(f32[1,4,256]{2,1,0:T(4,128)S(1)} %get-tuple-element.13), channel_id=1, source_target_pairs={{0,1},{1,0},{2,3},{3,2},{4,5},{5,4},{6,7},{7,6},{8,9},{9,8},{10,11... | collective-permute-start | bytes 12296 | tf_op jit(solution)/shard_map/ppermute | solution.py:478
  4.2 7.2 %collective-permute-start.1 = (f32[2,4,256]{2,1,0:T(4,128)S(1)}, f32[2,4,256]{2,1,0:T(4,128)S(1)}, u32[]{:S(2)}, u32[]{:S(2)}) collective-permute-start(f32[2,4,256]{2,1,0:T(4,128)S(1)} %constant_dynamic-update-slice_fusion.refs_1_.refs_5_), channel_id=1, source_target_pairs={{0,2},{2,0},{1,3},{3,1},{4,6},{6,4},{5,7},{7,5},{8,10},{10,8},{9,1... | collective-permute-start | bytes 24584 | tf_op jit(solution)/shard_map/ppermute | solution.py:478
  11.5 3.8 %collective-permute-start.2 = (f32[4,4,256]{2,1,0:T(4,128)S(1)}, f32[4,4,256]{2,1,0:T(4,128)S(1)}, u32[]{:S(2)}, u32[]{:S(2)}) collective-permute-start(f32[4,4,256]{2,1,0:T(4,128)S(1)} %pad_maximum_fusion.1), channel_id=1, source_target_pairs={{0,4},{4,0},{8,12},{12,8},{1,5},{5,1},{9,13},{13,9},{2,6},{6,2},{1... | collective-permute-start | bytes 49160 | tf_op jit(solution)/shard_map/ppermute | solution.py:478
  15.3 4.9 %collective-permute-start.3 = (f32[8,4,256]{2,1,0:T(4,128)S(1)}, f32[8,4,256]{2,1,0:T(4,128)S(1)}, u32[]{:S(2)}, u32[]{:S(2)}) collective-permute-start(f32[8,4,256]{2,1,0:T(4,128)S(1)} %pad_maximum_fusion), channel_id=1, source_target_pairs={{0,8},{4,12},{8,0},{12,4},{1,9},{5,13},{9,1},{13,5},{2,10},{6,14},... | collective-permute-start | bytes 98312 | tf_op jit(solution)/shard_map/ppermute | solution.py:478
  23.5 1.7 %collective-permute-start.4 = (f32[8,128]{1,0:T(8,128)S(1)}, f32[8,128]{1,0:T(8,128)S(1)}, u32[]{:S(2)}, u32[]{:S(2)}) collective-permute-start(f32[8,128]{1,0:T(8,128)S(1)} %get-tuple-element.21.refs_5_), channel_id=1, source_target_pairs={{0,1},{1,0},{2,3},{3,2},{4,5},{5,4},{6,7},{7,6},{8,9},{9,8},{10,11... | collective-permute-start | bytes 12296 | tf_op jit(solution)/shard_map/ppermute | solution.py:507
  25.2 3.6 %collective-permute-start.5 = (f32[8,128]{1,0:T(8,128)S(1)}, f32[8,128]{1,0:T(8,128)S(1)}, u32[]{:S(2)}, u32[]{:S(2)}) collective-permute-start(f32[8,128]{1,0:T(8,128)S(1)} %add.19.refs_5_), channel_id=1, source_target_pairs={{0,2},{2,0},{1,3},{3,1},{4,6},{6,4},{5,7},{7,5},{8,10},{10,8},{9,1... | collective-permute-start | bytes 12296 | tf_op jit(solution)/shard_map/ppermute | solution.py:507
  28.8 3.6 %collective-permute-start.6 = (f32[8,128]{1,0:T(8,128)S(1)}, f32[8,128]{1,0:T(8,128)S(1)}, u32[]{:S(2)}, u32[]{:S(2)}) collective-permute-start(f32[8,128]{1,0:T(8,128)S(1)} %add.20.refs_5_), channel_id=1, source_target_pairs={{0,4},{4,0},{8,12},{12,8},{1,5},{5,1},{9,13},{13,9},{2,6},{6,2},{1... | collective-permute-start | bytes 12296 | tf_op jit(solution)/shard_map/ppermute | solution.py:507
  32.5 4.5 %collective-permute-start.7 = (f32[8,128]{1,0:T(8,128)S(1)}, f32[8,128]{1,0:T(8,128)S(1)}, u32[]{:S(2)}, u32[]{:S(2)}) collective-permute-start(f32[8,128]{1,0:T(8,128)S(1)} %add.21.refs_5_.refs_0_), channel_id=1, source_target_pairs={{0,8},{4,12},{8,0},{12,4},{1,9},{5,13},{9,1},{13,5},{2,10},{6,14},... | collective-permute-start | bytes 12296 | tf_op jit(solution)/shard_map/ppermute | solution.py:507

commit v2 on v1

--- a/solution.py
+++ b/solution.py
@@ -14,6 +14,8 @@
 BQ = 256
 LEVELS = 4
 GROUPS = ((0, 1), (2, 3))
+
+SHARES = (0, 0.4, 0.3, 0.3)
 
 spread_width = 1.25
 exponent = -0.5 / spread_width**2 * math.log2(math.e)
@@ -99,18 +101,26 @@
     return jnp.where((node >= 0) & (node <= last), value, 0.0)
 
 
-def edge_hat(plan, shape, row_dim):
-    row = lax.broadcasted_iota(jnp.int32, shape, row_dim)
-    column = lax.broadcasted_iota(jnp.int32, shape, 1 - row_dim)
+def edge_hat(plan):
+    rows_x = plan.rows[0]
+    columns = round_up(plan.total - plan.main_rows, 128)
+    shape = (rows_x, columns)
+    point = lax.broadcasted_iota(jnp.int32, shape, 0)
+    column = lax.broadcasted_iota(jnp.int32, shape, 1)
     value = jnp.zeros(shape, jnp.float32)
+    shape = (8, columns)
+    row = lax.broadcasted_iota(jnp.int32, shape, 0)
+    other = lax.broadcasted_iota(jnp.int32, shape, 1)
+    mask = jnp.zeros(shape, jnp.float32)
     for level in range(LEVELS):
         cells = plan.cells[level][0]
-        node = column - (plan.off_edge[level] - plan.main_rows)
-        apart = (node * plan.rows[0] - (row >> 3) * cells).astype(jnp.float32)
-        one = jnp.maximum(0.0, 1.0 - jnp.abs(apart / plan.rows[0]))
-        here = ((row & 7) == level) & (node >= 0) & (node <= cells)
-        value = jnp.where(here, one, value)
-    return value
+        first = plan.off_edge[level] - plan.main_rows
+        apart = ((column - first) * rows_x - point * cells).astype(jnp.float32) / rows_x
+        one = jnp.maximum(0.0, 1.0 - jnp.abs(apart))
+        value = jnp.where((column >= first) & (column <= first + cells), one, value)
+        here = (row == level) & (other >= first) & (other <= first + cells)
+        mask = jnp.where(here, 1.0, mask)
+    return (value[:, None, :] * mask[None]).reshape(rows_x * 8, columns)
 
 
 def hats_kernel(plan, hat_y, hat_y_turned, hat_z, hat_z_turned, hat_x, hat_x_turned):
@@ -147,26 +157,19 @@
             hat_y_turned[...] = jnp.concatenate([whole, whole], axis=1)
         else:
             hat_y[...] = whole
-    hat_x[...] = edge_hat(plan, hat_x.shape, 0).astype(jnp.bfloat16)
-    hat_x_turned[...] = edge_hat(plan, hat_x_turned.shape, 1).astype(jnp.bfloat16)
-
-
-def prepare_kernel(packed, mine, consts):
-    blocks = mine.shape[0]
+    edges = edge_hat(plan)
+    count = plan.total - plan.main_rows
+    hat_x[...] = edges[:, :count].astype(jnp.bfloat16)
+    hat_x_turned[...] = edges.T[:count].astype(jnp.bfloat16)
+
+
+def prepare_kernel(raw, mine):
     slot = lax.broadcasted_iota(jnp.int32, (1, BQ), 1).astype(jnp.float32)
-    for block in range(blocks):
+    for block in range(mine.shape[0]):
         columns = slice(block * BQ, (block + 1) * BQ)
-        live = packed[5:6, block : block + 1]
-        mine[block, 0:1] = jnp.where(slot < live, packed[0:1, columns], 0.0)
-        mine[block, 1:4] = packed[1:4, columns]
-    shape = (1, consts.shape[1])
-    for level in range(LEVELS):
-        consts[level : level + 1] = jnp.broadcast_to(packed[4:5, level : level + 1], shape)
-    for axis in range(3):
-        consts[LEVELS + axis : LEVELS + axis + 1] = jnp.broadcast_to(
-            packed[6:7, axis : axis + 1], shape
-        )
-    consts[LEVELS + 3 :] = jnp.zeros(shape, jnp.float32)
+        live = slot < raw[4:5, block : block + 1]
+        mine[block, 0:1] = jnp.where(live, raw[0:1, columns], 0.0)
+        mine[block, 1:4] = raw[1:4, columns]
 
 
 def finish_kernel(scale, energy, got, out):
@@ -182,16 +185,27 @@
     return jnp.exp2(apart * apart * exponent)
 
 
+def fold(value):
+    while value.shape[0] > 1:
+        half = value.shape[0] // 2
+        both = value[:half] + value[half : 2 * half]
+        if value.shape[0] % 2:
+            first = both[:1] + value[2 * half :]
+            both = jnp.concatenate([first, both[1:]], axis=0) if half > 1 else first
+        value = both
+    return value[0]
+
+
 def spread_kernel(plan, together, first, last, *refs):
     refs = list(refs)
-    consts, charges = refs[:2]
+    index, charges = refs[:2]
     before = None if first else refs[2]
     turned = refs[2 if first else 3] if last else None
     outs = refs[2 + (not first) + last :]
     if last:
         energy = outs.pop(1)
     grids, along_x, along_y, along_z, planes = outs
-    begin = [consts[LEVELS + axis : LEVELS + axis + 1, :1] for axis in range(3)]
+    begin = [index[axis : axis + 1, :1] for axis in range(3)]
     steps = charges.shape[0] // together
 
     def one_step(step, before):
@@ -250,10 +264,7 @@
     else:
         lax.fori_loop(1, steps, lambda step, _: one_step(step, grids), None)
     if last:
-        rows = plan.total // 8
-        energy[...] = jnp.sum(
-            (grids[...] * turned[...]).reshape(rows, 8, plan.width), axis=0
-        )
+        energy[...] = fold((grids[...] * turned[...]).reshape(-1, 8, plan.width))
 
 
 def hat_terms(points, cells):
@@ -267,7 +278,7 @@
 
 
 def turned_kernel(
-    plan, density, scales, hat_y_turned, hat_z_turned, hat_x_turned, unused, out,
+    plan, density, amplitude, hat_y_turned, hat_z_turned, hat_x_turned, unused, out,
     held, along_y, along_x, sems,
 ):
     rows_x = plan.rows[0]
@@ -316,7 +327,7 @@
             slice(edge, edge + plan.pad_x[level]),
         ):
             value = jnp.concatenate(split(along_x[rows]), axis=1)
-            out[rows] = dot(value, hat_z_turned[level]) * scales[level : level + 1, :1]
+            out[rows] = dot(value, hat_z_turned[level]) * amplitude[:, level : level + 1]
     for group, levels in enumerate(GROUPS):
         at = plan.off_edge[levels[1]] + plan.pad_x[levels[1]]
         end = plan.off_edge[levels[0]] + plan.edge_rows[group]
@@ -324,16 +335,13 @@
             out[at:end] = jnp.zeros((end - at, plan.width), jnp.float32)
 
 
-def field_kernel(plan, part, parts, *refs):
-    grids, scales, hat_y, hat_z, hat_x = refs[:5]
-    field, drawn = refs[-2:]
-    rows_x = plan.rows[0]
-    count = rows_x // parts
-    planes = range(part * count, (part + 1) * count)
-    terms = [hat_terms(rows_x, cells[0]) for cells in plan.cells]
+def field_kernel(plan, planes, chunk, *refs):
+    grids, amplitude, hat_y, hat_z, hat_x = refs[:5]
+    field, drawn, held, sems = refs[-4:]
+    terms = [hat_terms(plan.rows[0], cells[0]) for cells in plan.cells]
 
     def interpolate_z(level, rows):
-        value = jnp.concatenate(split(grids[rows] * scales[level : level + 1, : plan.width]), axis=1)
+        value = jnp.concatenate(split(grids[rows] * amplitude[:, level : level + 1]), axis=1)
         drawn[rows] = dot(value, hat_z[level])
 
     for level in range(LEVELS):
@@ -350,6 +358,7 @@
     rows = slice(planes[0] * 8, (planes[-1] + 1) * 8)
     edges = dot(hat_x[rows], high) + dot(hat_x[rows], low)
     rest = plan.stack - plan.off_stack[-1] - 8
+    copies = []
     for plane in planes[::2]:
         both = []
         for one in (plane, plane + 1):
@@ -368,16 +377,35 @@
                 stack.append(jnp.zeros((rest, drawn.shape[1]), jnp.float32))
             both.append(jnp.concatenate(stack, axis=0))
         value = dot(hat_y[...], jnp.concatenate(both, axis=1).astype(jnp.bfloat16))
-        field[plane - planes[0]] = value[:, : plan.rows[2]]
-        field[plane + 1 - planes[0]] = value[:, plan.rows[2] :]
-
-
-def rounds(order):
-    for axis in order:
-        peers = lax.axis_size(axis)
+        at = plane - planes[0]
+        held[at] = value[:, : plan.rows[2]]
+        held[at + 1] = value[:, plan.rows[2] :]
+        at += 2
+        if at % chunk == 0 or at == len(planes):
+            size = chunk if at % chunk == 0 else at % chunk
+            copy = pltpu.make_async_copy(
+                held.at[pl.ds(at - size, size)],
+                field.at[pl.ds(planes[0] + at - size, size)],
+                sems.at[len(copies)],
+            )
+            copy.start()
+            copies.append(copy)
+    for copy in copies:
+        copy.wait()
+
+
+def rounds():
+    cores = lax.axis_size("sub")
+    yield "sub", [(core, core ^ 1) for core in range(cores)]
+    for axis in ("blk", "slab"):
+        chips = lax.axis_size(axis)
         by = 1
-        while by < peers:
-            yield axis, [(i, i ^ by) for i in range(peers)]
+        while by < chips:
+            yield (axis, "sub"), [
+                (chip * cores + core, (chip ^ by) * cores + (core ^ 1))
+                for chip in range(chips)
+                for core in range(cores)
+            ]
             by *= 2
 
 
@@ -386,8 +414,7 @@
     rows = density.shape
     axes = ("slab", "blk", "sub")
     plan = Plan(tuple(count * lax.axis_size(axis) for count, axis in zip(rows, axes)), rows)
-    order = ("sub", "blk", "slab")
-    steps = list(rounds(order))
+    steps = list(rounds())
     f32, bf16 = jnp.float32, jnp.bfloat16
 
     hats = pl.pallas_call(
@@ -404,44 +431,32 @@
             )
         ],
         out_specs=[vmem] * 6,
+        cost_estimate=pl.CostEstimate(flops=15 * 10**8, bytes_accessed=0, transcendentals=0),
         compiler_params=params,
         name="hats",
     )()
     hat_y, hat_y_turned, hat_z, hat_z_turned, hat_x, hat_x_turned = hats
+    amplitude = level_amplitude.reshape(1, LEVELS)
 
     slots = blocks * BQ
     row = lax.broadcasted_iota(jnp.int32, (8, slots), 0)
-    column = lax.broadcasted_iota(jnp.int32, (8, slots), 1)
-
-    def wide(vector):
-        return jnp.pad(vector.astype(f32), (0, slots - vector.shape[0]))[None, :]
-
-    index = [lax.axis_index(axis).astype(f32) for axis in axes]
-    index = jnp.where(column == 0, index[0], jnp.where(column == 1, index[1], index[2]))
-    places = jnp.where(row == 1, cell_x[None], jnp.where(row == 2, cell_y[None], cell_z[None]))
-    places = places.astype(f32) + jnp.pad(offsets, ((1, 4), (0, 0)))
-    packed = jnp.where(
-        row == 0,
-        charge[None],
-        jnp.where(
-            row < 4,
-            places,
-            jnp.where(
-                row == 4, wide(level_amplitude), jnp.where(row == 5, wide(block_count), index)
-            ),
-        ),
-    )
-    mine, consts = pl.pallas_call(
+    counts = lax.dynamic_update_slice(jnp.zeros((slots,), jnp.int32), block_count, (0,))
+    whole = jnp.where(row == 1, cell_x[None], jnp.where(row == 2, cell_y[None], cell_z[None]))
+    whole = jnp.where(row == 4, counts[None], whole)
+    raw = whole.astype(f32) + jnp.pad(offsets, ((1, 4), (0, 0)))
+    raw = jnp.where(row == 0, charge[None], raw)
+    mine = pl.pallas_call(
         prepare_kernel,
-        out_shape=[
-            jax.ShapeDtypeStruct((blocks, 4, BQ), f32),
-            jax.ShapeDtypeStruct((8, 128), f32),
-        ],
+        out_shape=jax.ShapeDtypeStruct((blocks, 4, BQ), f32),
         in_specs=[vmem],
-        out_specs=[vmem] * 2,
+        out_specs=vmem,
+        cost_estimate=pl.CostEstimate(flops=15 * 10**8, bytes_accessed=0, transcendentals=0),
         compiler_params=params,
         name="prepare",
-    )(packed)
+    )(raw)
+    index = [lax.axis_index(axis).astype(f32) for axis in axes]
+    row = lax.broadcasted_iota(jnp.int32, (8, 128), 0)
+    begin = jnp.where(row == 0, index[0], jnp.where(row == 1, index[1], index[2]))
 
     grid_shape = jax.ShapeDtypeStruct((plan.total, plan.width), f32)
 
@@ -450,7 +465,7 @@
         together = math.gcd(count, 4)
         deep = together * BQ
         first, last = before is None, turned is not None
-        operands = [consts, charges] + [x for x in (before, turned) if x is not None]
+        operands = [begin, charges] + [x for x in (before, turned) if x is not None]
         return pl.pallas_call(
             lambda *refs: spread_kernel(plan, together, first, last, *refs),
             out_shape=[grid_shape] + [jax.ShapeDtypeStruct((8, plan.width), f32)] * last,
@@ -468,6 +483,33 @@
             ),
             compiler_params=params,
             name="spread",
+        )(*operands)
+
+    def draw(grids, energy, field, planes):
+        operands = [grids, amplitude, hat_y, hat_z, hat_x, energy]
+        specs = [vmem] * len(operands)
+        if field is not None:
+            operands.append(field)
+            specs.append(hbm)
+        chunk = 8
+        return pl.pallas_call(
+            lambda *refs: field_kernel(plan, planes, chunk, *refs),
+            out_shape=jax.ShapeDtypeStruct(rows, f32),
+            in_specs=specs,
+            out_specs=hbm,
+            scratch_shapes=[
+                pltpu.VMEM((plan.total, rows[2]), f32),
+                pltpu.VMEM((len(planes), rows[1], rows[2]), f32),
+                pltpu.SemaphoreType.DMA((-(-len(planes) // chunk),)),
+            ],
+            input_output_aliases={} if field is None else {len(operands) - 1: 0},
+            cost_estimate=pl.CostEstimate(
+                flops=10**9,
+                bytes_accessed=len(planes) * rows[1] * rows[2] * 4,
+                transcendentals=0,
+            ),
+            compiler_params=params,
+            name="field",
         )(*operands)
 
     parts = math.gcd(4, rows[0] // 2)
@@ -492,41 +534,25 @@
                 cost_estimate=pl.CostEstimate(
                     flops=2 * 10**9, bytes_accessed=math.prod(rows) * 4, transcendentals=0
                 ),
-                compiler_params=pltpu.CompilerParams(vmem_limit_bytes=51 * 2**20),
+                compiler_params=pltpu.CompilerParams(vmem_limit_bytes=48 * 2**20),
                 name="turned",
-            )(density, consts, hat_y_turned, hat_z_turned, hat_x_turned, held)
-        new = held if number == 0 else got
-        end = number == len(steps) - 1
-        out = spread(new, grids, turned if end else None)
-        grids = out[0]
+            )(density, amplitude, hat_y_turned, hat_z_turned, hat_x_turned, held)
+        if number:
+            end = number == len(steps) - 1
+            out = spread(held if number == 1 else got, grids, turned if end else None)
+            grids = out[0]
     energy = out[1]
 
-    count = rows[0] // parts
     field = None
+    bounds = [0]
+    for number in range(len(steps)):
+        done = 1.0 if number == len(steps) - 1 else sum(SHARES[: number + 1])
+        bounds.append(2 * round(rows[0] // 2 * min(done, 1.0)))
     for number, (axis, pairs) in enumerate(steps):
         got = lax.ppermute(energy, axis, pairs)
-        if number < parts:
-            operands = [grids, consts, hat_y, hat_z, hat_x, energy]
-            specs = [vmem] * len(operands)
-            if field is not None:
-                operands.append(field)
-                specs.append(hbm)
-            field = pl.pallas_call(
-                lambda *refs, part=number: field_kernel(plan, part, parts, *refs),
-                grid=(1,),
-                out_shape=jax.ShapeDtypeStruct(rows, f32),
-                in_specs=specs,
-                out_specs=pl.BlockSpec(
-                    (count, rows[1], rows[2]), lambda i, part=number: (part, 0, 0)
-                ),
-                scratch_shapes=[pltpu.VMEM((plan.total, rows[2]), f32)],
-                input_output_aliases={} if field is None else {len(operands) - 1: 0},
-                cost_estimate=pl.CostEstimate(
-                    flops=10**9, bytes_accessed=math.prod(rows) * 4 // parts, transcendentals=0
-                ),
-                compiler_params=params,
-                name="field",
-            )(*operands)
+        if bounds[number] < bounds[number + 1]:
+            planes = range(bounds[number], bounds[number + 1])
+            field = draw(grids, energy, field, planes)
         if number < len(steps) - 1:
             energy = energy + got
     fine = math.prod(count * lax.axis_size(axis) for count, axis in zip(rows, axes))

time: 37.7 us -> 33 us (0.88)
  Pallas kernels: 18.7 us -> 15.8 us
  waiting for transfers between devices: 3.9 us -> 1.3 us
  starting transfers between devices: 12 us -> 13.3 us
  local copies, waits for them, and re-layouts: 0.68 us -> 0.01 us
    ppermute x4, starting transfers between devices: 4.47 us -> 6.06 us  [on_device(): got = lax.ppermute(energy, axis, pairs)]
    ppermute x4, waiting for transfers between devices: 2.42 us -> 0.96 us  [on_device(): got = lax.ppermute(energy, axis, pairs)]
    ppermute x4, waiting for transfers between devices: 1.48 us -> 0.34 us  [on_device(): got = lax.ppermute(held, axis, pairs)]
    pallas_call x5 -> x4, Pallas kernels: 6.61 us -> 5.56 us  [the longest x3 5.48 us: draw(): pl.pallas_call(lambda *refs: field_kernel(plan, planes, chunk, *refs), ou...]
    pallas_call x1, Pallas kernels: 3.44 us -> 2.52 us  [on_device(): pl.pallas_call(lambda *refs: turned_kernel(plan, *refs), out_shape=grid_s...]
    pad x2 -> x0, local copies, waits for them, and re-layouts: 0.67 us -> none  [wide(): return jnp.pad(vector.astype(f32), (0, slots - vector.shape[0]))[None, :]]
    pallas_call x1, Pallas kernels: 0.84 us -> 0.4 us  [on_device(): pl.pallas_call(lambda *refs: hats_kernel(plan, *refs), out_shape=[jax.Sha...]
    pallas_call x4 -> x3, Pallas kernels: 7.2 us -> 6.76 us  [spread(): pl.pallas_call(lambda *refs: spread_kernel(plan, together, first, last, *...]
  transfers between devices with their start and end apart: 8 -> 8, of which waited for: 5 -> 2; matrix products, arithmetic and copies ran while one was open for 0% -> 0% of each run, Pallas kernels for 39% -> 36%
where the time goes in v2:
time: 33 us; the launch traced here: 32.8 us
  Pallas kernels  15.8 us (48%)
  starting transfers between devices  13.3 us (40%)
  between operations  1.43 us (4%)
  waiting for transfers between devices  1.3 us (4%)
  other arithmetic  0.95 us (3%)
    ppermute x4, starting transfers between devices, on_device(): got = lax.ppermute(held, axis, pairs)  7.21 us
    pallas_call x3, Pallas kernels, spread(): pl.pallas_call(lambda *refs: spread_kernel(plan, together, first, last, *...  6.76 us
    ppermute x4, starting transfers between devices, on_device(): got = lax.ppermute(energy, axis, pairs)  6.06 us
    pallas_call x3, Pallas kernels, draw(): pl.pallas_call(lambda *refs: field_kernel(plan, planes, chunk, *refs), ou...  5.48 us
    pallas_call x1, Pallas kernels, on_device(): pl.pallas_call(lambda *refs: turned_kernel(plan, *refs), out_shape=grid_s...  2.52 us
    ppermute x4, waiting for transfers between devices, on_device(): got = lax.ppermute(energy, axis, pairs)  0.96 us
    select_n x1, other arithmetic, on_device(): raw = jnp.where(row == 0, charge[None], raw)  0.82 us
  transfers between devices with their start and end apart: 8, of which 2 were waited for; matrix products, arithmetic and copies ran while one was open for 0% of the time, Pallas kernels for 36%

profile of v2, /device:TPU:0, one launch (start us, length us, event | category | flops | bytes accessed | tf_op | source)
XLA Modules:
  0.0 32.8 jit_solution(13414401828497968664)
XLA Ops:
  1.3 0.8 %add_select_fusion.raw = f32[8,256]{1,0:T(8,128)S(1)} fusion(f32[3,256]{1,0:T(4,128)} %param.11, s32[256]{0:T(256)} %param.10, s32[256]{0:T(256)} %param.9, s32[256]{0:T(256)} %param.8, s32[256]{0:T(256)S(1)} %dynamic_update_slice.3, f32[256]{0:T(256)} %param.12, pred[8]{0:T(512)(128)(4,1)S(1)} %get-tuple-element.18, pred[8]{0:T(512)(128)(4,1)S(1)} %get-tuple-element.20, ...), kind=kLoop, calls=%fused_computation.3 | loop fusion | flops 12288 | bytes 16416 | tf_op jit(solution)/shard_map/jit(_where)/select_n | solution.py:447
  2.1 0.0 copy-start
  2.1 0.1 prepare.1
  2.2 0.5 %collective-permute-start = (f32[1,4,256]{2,1,0:T(4,128)S(1)}, f32[1,4,256]{2,1,0:T(4,128)S(1)}, u32[]{:S(2)}, u32[]{:S(2)}) collective-permute-start(f32[1,4,256]{2,1,0:T(4,128)S(1)} %prepare.1), channel_id=1, source_target_pairs={{0,1},{1,0},{2,3},{3,2},{4,5},{5,4},{6,7},{7,6},{8,9},{9,8},{10,11... | collective-permute-start | bytes 12296 | tf_op jit(solution)/shard_map/ppermute | solution.py:520
  2.7 0.0 copy-start.1
  2.7 0.1 broadcast_select_fusion.refs_0_
  2.8 0.4 %hats.1 = (bf16[128,176]{1,0:T(8,128)(2,1)S(1)}, bf16[176,256]{1,0:T(8,128)(2,1)S(1)}, bf16[4,256,128]{2,1,0:T(8,128)(2,1)S(1)}, bf16[4,256,128]{2,1,0:T(8,128)(...) custom-call(), custom_call_target="tpu_custom_call" | custom-call | flops 1500000000 | tf_op jit(solution)/shard_map/hats/pallas_call | solution.py:420
  3.2 0.3 %collective-permute-done = f32[1,4,256]{2,1,0:T(4,128)S(1)} collective-permute-done((f32[1,4,256]{2,1,0:T(4,128)S(1)}, f32[1,4,256]{2,1,0:T(4,128)S(1)}, u32[]{:S(2)}, u32[]{:S(2)}) %collective-permute-start) | collective-permute-done | bytes 4128 | tf_op jit(solution)/shard_map/ppermute | solution.py:520
  3.5 2.6 %collective-permute-start.1 = (f32[2,4,256]{2,1,0:T(4,128)S(1)}, f32[2,4,256]{2,1,0:T(4,128)S(1)}, u32[]{:S(2)}, u32[]{:S(2)}) collective-permute-start(f32[2,4,256]{2,1,0:T(4,128)S(1)} %pad_maximum_fusion.2.refs_5_), channel_id=1, source_target_pairs={{0,3},{1,2},{2,1},{3,0},{4,7},{5,6},{6,5},{7,4},{8,11},{9,10},{10,... | collective-permute-start | bytes 24584 | tf_op jit(solution)/shard_map/ppermute | solution.py:520
  6.1 0.0 copy-done
  6.1 0.0 copy-done.1
  6.1 2.5 %turned.1.refs_3_ = f32[2160,128]{1,0:T(8,128)S(1)} custom-call(f32[64,128,128]{2,1,0:T(8,128)S(1)} %copy-done.1, f32[1,4]{1,0:T(1,128)S(1)} %bitcast.2, bf16[176,256]{1,0:T(8,128)(2,1)S(1)} %get-tuple-element.10.refs_2_, bf16[4,256,128]{2,1,0:T(8,128)(2,1)S(1)} %get-tuple-element.11.refs_3_, bf16[80,512]{1,0:T(8,128)(2,1)S(1)} %get-tuple-element.12.refs_4_, ...), custom_call_target="tpu_custom_call" | custom-call | flops 2000000000 | bytes 4194304 | tf_op jit(solution)/shard_map/turned/pallas_call | solution.py:523
  8.6 0.0 collective-permute-done.1
  8.7 1.6 %collective-permute-start.2 = (f32[4,4,256]{2,1,0:T(4,128)S(1)}, f32[4,4,256]{2,1,0:T(4,128)S(1)}, u32[]{:S(2)}, u32[]{:S(2)}) collective-permute-start(f32[4,4,256]{2,1,0:T(4,128)S(1)} %pad_maximum_fusion.1.refs_1_), channel_id=1, source_target_pairs={{0,5},{1,4},{4,1},{5,0},{8,13},{9,12},{12,9},{13,8},{2,7},{3,6},{6... | collective-permute-start | bytes 49160 | tf_op jit(solution)/shard_map/ppermute | solution.py:520
  10.3 1.7 %spread.3.refs_2_ = f32[2160,128]{1,0:T(8,128)S(1)} custom-call(f32[8,128]{1,0:T(8,128)S(1)} %broadcast_select_fusion.refs_0_, f32[4,4,256]{2,1,0:T(4,128)S(1)} %pad_maximum_fusion.1.refs_1_), custom_call_target="tpu_custom_call" | custom-call | flops 1132462080 | tf_op jit(solution)/shard_map/spread/pallas_call | solution.py:469
  11.9 0.0 collective-permute-done.2.refs_1_
  12.0 2.6 %collective-permute-start.3 = (f32[8,4,256]{2,1,0:T(4,128)S(1)}, f32[8,4,256]{2,1,0:T(4,128)S(1)}, u32[]{:S(2)}, u32[]{:S(2)}) collective-permute-start(f32[8,4,256]{2,1,0:T(4,128)S(1)} %pad_maximum_fusion), channel_id=1, source_target_pairs={{0,9},{1,8},{4,13},{5,12},{8,1},{9,0},{12,5},{13,4},{2,11},{3,10},... | collective-permute-start | bytes 98312 | tf_op jit(solution)/shard_map/ppermute | solution.py:520
  14.5 1.8 %spread.4.refs_2_ = f32[2160,128]{1,0:T(8,128)S(1)} custom-call(f32[8,128]{1,0:T(8,128)S(1)} %broadcast_select_fusion.refs_0_, f32[4,4,256]{2,1,0:T(4,128)S(1)} %collective-permute-done.2.refs_1_, f32[2160,128]{1,0:T(8,128)S(1)} %spread.3.refs_2_), custom_call_target="tpu_custom_call", output_to_operand_aliasing={{}: (2, {})} | custom-call | flops 1132462080 | tf_op jit(solution)/shard_map/spread/pallas_call | solution.py:469
  16.3 0.0 collective-permute-done.3.refs_1_
  16.4 3.3 %spread.5 = (f32[2160,128]{1,0:T(8,128)S(1)}, f32[8,128]{1,0:T(8,128)S(1)}) custom-call(f32[8,128]{1,0:T(8,128)S(1)} %broadcast_select_fusion.refs_0_, f32[8,4,256]{2,1,0:T(4,128)S(1)} %collective-permute-done.3.refs_1_, f32[2160,128]{1,0:T(8,128)S(1)} %spread.4.refs_2_, f32[2160,128]{1,0:T(8,128)S(1)} %turned.1.refs_3_), custom_call_target="tpu_custom_call", output_to_operand_aliasing={{0}: (2, {})} | custom-call | flops 2264924160 | tf_op jit(solution)/shard_map/spread/pallas_call | solution.py:469
  19.6 0.3 collective-permute-start.4
  19.9 1.0 %collective-permute-done.4 = f32[8,128]{1,0:T(8,128)S(1)} collective-permute-done((f32[8,128]{1,0:T(8,128)S(1)}, f32[8,128]{1,0:T(8,128)S(1)}, u32[]{:S(2)}, u32[]{:S(2)}) %collective-permute-start.4) | collective-permute-done | bytes 4128 | tf_op jit(solution)/shard_map/ppermute | solution.py:552
  20.9 1.2 %collective-permute-start.5 = (f32[8,128]{1,0:T(8,128)S(1)}, f32[8,128]{1,0:T(8,128)S(1)}, u32[]{:S(2)}, u32[]{:S(2)}) collective-permute-start(f32[8,128]{1,0:T(8,128)S(1)} %add.17.refs_5_), channel_id=1, source_target_pairs={{0,3},{1,2},{2,1},{3,0},{4,7},{5,6},{6,5},{7,4},{8,11},{9,10},{10,... | collective-permute-start | bytes 12296 | tf_op jit(solution)/shard_map/ppermute | solution.py:552
  22.1 2.0 %field.3.refs_6_ = f32[64,128,128]{2,1,0:T(8,128)} custom-call(f32[2160,128]{1,0:T(8,128)S(1)} %get-tuple-element.13.refs_0_, f32[1,4]{1,0:T(1,128)S(1)} %bitcast.3, bf16[128,176]{1,0:T(8,128)(2,1)S(1)} %get-tuple-element.14.refs_2_, bf16[4,256,128]{2,1,0:T(8,128)(2,1)S(1)} %get-tuple-element.15.refs_3_, bf16[512,80]{1,0:T(8,128)(2,1)S(1)} %get-tuple-element.16.refs_4_, ...), custom_call_target="tpu_custom_call" | custom-call | flops 1000000000 | bytes 1703936 | tf_op jit(solution)/shard_map/field/pallas_call | solution.py:495
  24.1 0.0 collective-permute-done.5
  24.1 1.6 %collective-permute-start.6 = (f32[8,128]{1,0:T(8,128)S(1)}, f32[8,128]{1,0:T(8,128)S(1)}, u32[]{:S(2)}, u32[]{:S(2)}) collective-permute-start(f32[8,128]{1,0:T(8,128)S(1)} %add.18.refs_5_), channel_id=1, source_target_pairs={{0,5},{1,4},{4,1},{5,0},{8,13},{9,12},{12,9},{13,8},{2,7},{3,6},{6... | collective-permute-start | bytes 12296 | tf_op jit(solution)/shard_map/ppermute | solution.py:552
  25.7 1.7 %field.4.refs_6_ = f32[64,128,128]{2,1,0:T(8,128)} custom-call(f32[2160,128]{1,0:T(8,128)S(1)} %get-tuple-element.13.refs_0_, f32[1,4]{1,0:T(1,128)S(1)} %bitcast.4, bf16[128,176]{1,0:T(8,128)(2,1)S(1)} %get-tuple-element.14.refs_2_, bf16[4,256,128]{2,1,0:T(8,128)(2,1)S(1)} %get-tuple-element.15.refs_3_, ...), custom_call_target="tpu_custom_call", output_to_operand_aliasing={{}: (6, {})} | custom-call | flops 1000000000 | bytes 1179648 | tf_op jit(solution)/shard_map/field/pallas_call | solution.py:495
  27.4 0.0 collective-permute-done.6
  27.5 3.0 %collective-permute-start.7 = (f32[8,128]{1,0:T(8,128)S(1)}, f32[8,128]{1,0:T(8,128)S(1)}, u32[]{:S(2)}, u32[]{:S(2)}) collective-permute-start(f32[8,128]{1,0:T(8,128)S(1)} %add.19.refs_5_.refs_0_), channel_id=1, source_target_pairs={{0,9},{1,8},{4,13},{5,12},{8,1},{9,0},{12,5},{13,4},{2,11},{3,10},... | collective-permute-start | bytes 12296 | tf_op jit(solution)/shard_map/ppermute | solution.py:552
  30.4 1.7 %field.5 = f32[64,128,128]{2,1,0:T(8,128)} custom-call(f32[2160,128]{1,0:T(8,128)S(1)} %get-tuple-element.13.refs_0_, f32[1,4]{1,0:T(1,128)S(1)} %bitcast.5, bf16[128,176]{1,0:T(8,128)(2,1)S(1)} %get-tuple-element.14.refs_2_, bf16[4,256,128]{2,1,0:T(8,128)(2,1)S(1)} %get-tuple-element.15.refs_3_, ...), custom_call_target="tpu_custom_call", output_to_operand_aliasing={{}: (6, {})} | custom-call | flops 1000000000 | bytes 1310720 | tf_op jit(solution)/shard_map/field/pallas_call | solution.py:495
  32.2 0.0 collective-permute-done.7.refs_1_
  32.2 0.6 %finish.1 = f32[1,1]{1,0:T(1,128)} custom-call(f32[8,128]{1,0:T(8,128)S(1)} %add.19.refs_5_.refs_0_, f32[8,128]{1,0:T(8,128)S(1)} %collective-permute-done.7.refs_1_), custom_call_target="tpu_custom_call" | custom-call | tf_op jit(solution)/shard_map/finish/pallas_call | solution.py:559
  (10 shorter events, 0.1 us)
Async XLA Ops:
  2.1 4.0 %copy-start = (f32[4]{0:T(128)S(1)}, f32[4]{0:T(128)}, u32[]{:S(2)}) copy-start(f32[4]{0:T(128)} %param.14) | copy-start | bytes 52
  2.2 1.3 %collective-permute-start = (f32[1,4,256]{2,1,0:T(4,128)S(1)}, f32[1,4,256]{2,1,0:T(4,128)S(1)}, u32[]{:S(2)}, u32[]{:S(2)}) collective-permute-start(f32[1,4,256]{2,1,0:T(4,128)S(1)} %prepare.1), channel_id=1, source_target_pairs={{0,1},{1,0},{2,3},{3,2},{4,5},{5,4},{6,7},{7,6},{8,9},{9,8},{10,11... | collective-permute-start | bytes 12296 | tf_op jit(solution)/shard_map/ppermute | solution.py:520
  2.7 3.4 %copy-start.1 = (f32[64,128,128]{2,1,0:T(8,128)S(1)}, f32[64,128,128]{2,1,0:T(8,128)}, u32[]{:S(2)}) copy-start(f32[64,128,128]{2,1,0:T(8,128)} %refs_0_.1) | copy-start | bytes 12582916
  3.5 5.1 %collective-permute-start.1 = (f32[2,4,256]{2,1,0:T(4,128)S(1)}, f32[2,4,256]{2,1,0:T(4,128)S(1)}, u32[]{:S(2)}, u32[]{:S(2)}) collective-permute-start(f32[2,4,256]{2,1,0:T(4,128)S(1)} %pad_maximum_fusion.2.refs_5_), channel_id=1, source_target_pairs={{0,3},{1,2},{2,1},{3,0},{4,7},{5,6},{6,5},{7,4},{8,11},{9,10},{10,... | collective-permute-start | bytes 24584 | tf_op jit(solution)/shard_map/ppermute | solution.py:520
  8.7 3.3 %collective-permute-start.2 = (f32[4,4,256]{2,1,0:T(4,128)S(1)}, f32[4,4,256]{2,1,0:T(4,128)S(1)}, u32[]{:S(2)}, u32[]{:S(2)}) collective-permute-start(f32[4,4,256]{2,1,0:T(4,128)S(1)} %pad_maximum_fusion.1.refs_1_), channel_id=1, source_target_pairs={{0,5},{1,4},{4,1},{5,0},{8,13},{9,12},{12,9},{13,8},{2,7},{3,6},{6... | collective-permute-start | bytes 49160 | tf_op jit(solution)/shard_map/ppermute | solution.py:520
  12.0 4.4 %collective-permute-start.3 = (f32[8,4,256]{2,1,0:T(4,128)S(1)}, f32[8,4,256]{2,1,0:T(4,128)S(1)}, u32[]{:S(2)}, u32[]{:S(2)}) collective-permute-start(f32[8,4,256]{2,1,0:T(4,128)S(1)} %pad_maximum_fusion), channel_id=1, source_target_pairs={{0,9},{1,8},{4,13},{5,12},{8,1},{9,0},{12,5},{13,4},{2,11},{3,10},... | collective-permute-start | bytes 98312 | tf_op jit(solution)/shard_map/ppermute | solution.py:520
  19.6 1.2 %collective-permute-start.4 = (f32[8,128]{1,0:T(8,128)S(1)}, f32[8,128]{1,0:T(8,128)S(1)}, u32[]{:S(2)}, u32[]{:S(2)}) collective-permute-start(f32[8,128]{1,0:T(8,128)S(1)} %get-tuple-element.17), channel_id=1, source_target_pairs={{0,1},{1,0},{2,3},{3,2},{4,5},{5,4},{6,7},{7,6},{8,9},{9,8},{10,11... | collective-permute-start | bytes 12296 | tf_op jit(solution)/shard_map/ppermute | solution.py:552
  20.9 3.2 %collective-permute-start.5 = (f32[8,128]{1,0:T(8,128)S(1)}, f32[8,128]{1,0:T(8,128)S(1)}, u32[]{:S(2)}, u32[]{:S(2)}) collective-permute-start(f32[8,128]{1,0:T(8,128)S(1)} %add.17.refs_5_), channel_id=1, source_target_pairs={{0,3},{1,2},{2,1},{3,0},{4,7},{5,6},{6,5},{7,4},{8,11},{9,10},{10,... | collective-permute-start | bytes 12296 | tf_op jit(solution)/shard_map/ppermute | solution.py:552
  24.1 3.3 %collective-permute-start.6 = (f32[8,128]{1,0:T(8,128)S(1)}, f32[8,128]{1,0:T(8,128)S(1)}, u32[]{:S(2)}, u32[]{:S(2)}) collective-permute-start(f32[8,128]{1,0:T(8,128)S(1)} %add.18.refs_5_), channel_id=1, source_target_pairs={{0,5},{1,4},{4,1},{5,0},{8,13},{9,12},{12,9},{13,8},{2,7},{3,6},{6... | collective-permute-start | bytes 12296 | tf_op jit(solution)/shard_map/ppermute | solution.py:552
  27.5 4.7 %collective-permute-start.7 = (f32[8,128]{1,0:T(8,128)S(1)}, f32[8,128]{1,0:T(8,128)S(1)}, u32[]{:S(2)}, u32[]{:S(2)}) collective-permute-start(f32[8,128]{1,0:T(8,128)S(1)} %add.19.refs_5_.refs_0_), channel_id=1, source_target_pairs={{0,9},{1,8},{4,13},{5,12},{8,1},{9,0},{12,5},{13,4},{2,11},{3,10},... | collective-permute-start | bytes 12296 | tf_op jit(solution)/shard_map/ppermute | solution.py:552

commit v3 on v2

--- a/solution.py
+++ b/solution.py
@@ -15,7 +15,8 @@
 LEVELS = 4
 GROUPS = ((0, 1), (2, 3))
 
-SHARES = (0, 0.4, 0.3, 0.3)
+
+SHARES = (0, 0.5, 0.25, 0.25)
 
 spread_width = 1.25
 exponent = -0.5 / spread_width**2 * math.log2(math.e)
@@ -396,17 +397,21 @@
 
 def rounds():
     cores = lax.axis_size("sub")
-    yield "sub", [(core, core ^ 1) for core in range(cores)]
+    found = []
     for axis in ("blk", "slab"):
-        chips = lax.axis_size(axis)
         by = 1
-        while by < chips:
-            yield (axis, "sub"), [
-                (chip * cores + core, (chip ^ by) * cores + (core ^ 1))
-                for chip in range(chips)
-                for core in range(cores)
-            ]
+        while by < lax.axis_size(axis):
+            found.append((axis, by))
             by *= 2
+    steps = [("sub", [(core, core ^ 1) for core in range(cores)])]
+    for axis, by in sorted(found, key=lambda step: -step[1]):
+        pairs = [
+            (chip * cores + core, (chip ^ by) * cores + (core ^ 1))
+            for chip in range(lax.axis_size(axis))
+            for core in range(cores)
+        ]
+        steps.append(((axis, "sub"), pairs))
+    return steps
 
 
 def on_device(cell_x, cell_y, cell_z, offsets, charge, block_count, level_amplitude, density):
@@ -414,7 +419,7 @@
     rows = density.shape
     axes = ("slab", "blk", "sub")
     plan = Plan(tuple(count * lax.axis_size(axis) for count, axis in zip(rows, axes)), rows)
-    steps = list(rounds())
+    steps = rounds()
     f32, bf16 = jnp.float32, jnp.bfloat16
 
     hats = pl.pallas_call(

time: 33 us -> 31.8 us (0.964)
  starting transfers between devices: 13.3 us -> 11.9 us
  waiting for transfers between devices: 1.3 us -> 1.69 us
    ppermute x4, starting transfers between devices: 6.06 us -> 4.66 us  [on_device(): got = lax.ppermute(energy, axis, pairs)]
  transfers between devices with their start and end apart: 8 -> 8, of which waited for: 2 -> 4; matrix products, arithmetic and copies ran while one was open for 0% -> 0% of each run, Pallas kernels for 36% -> 37%
where the time goes in v3:
time: 31.8 us; the launch traced here: 31.7 us
  Pallas kernels  15.7 us (49%)
  starting transfers between devices  11.9 us (37%)
  waiting for transfers between devices  1.69 us (5%)
  between operations  1.41 us (4%)
  other arithmetic  0.95 us (3%)
    ppermute x4, starting transfers between devices, on_device(): got = lax.ppermute(held, axis, pairs)  7.23 us
    pallas_call x3, Pallas kernels, spread(): pl.pallas_call(lambda *refs: spread_kernel(plan, together, first, last, *...  6.74 us
    pallas_call x3, Pallas kernels, draw(): pl.pallas_call(lambda *refs: field_kernel(plan, planes, chunk, *refs), ou...  5.37 us
    ppermute x4, starting transfers between devices, on_device(): got = lax.ppermute(energy, axis, pairs)  4.66 us
    pallas_call x1, Pallas kernels, on_device(): pl.pallas_call(lambda *refs: turned_kernel(plan, *refs), out_shape=grid_s...  2.54 us
    ppermute x4, waiting for transfers between devices, on_device(): got = lax.ppermute(energy, axis, pairs)  1.27 us
    select_n x1, other arithmetic, on_device(): raw = jnp.where(row == 0, charge[None], raw)  0.82 us
  transfers between devices with their start and end apart: 8, of which 4 were waited for; matrix products, arithmetic and copies ran while one was open for 0% of the time, Pallas kernels for 37%

profile of v3, /device:TPU:0, one launch (start us, length us, event | category | flops | bytes accessed | tf_op | source)
XLA Modules:
  0.0 31.7 jit_solution(3267422717984175066)
XLA Ops:
  1.3 0.8 %add_select_fusion.raw = f32[8,256]{1,0:T(8,128)S(1)} fusion(f32[3,256]{1,0:T(4,128)} %param.11, s32[256]{0:T(256)} %param.10, s32[256]{0:T(256)} %param.9, s32[256]{0:T(256)} %param.8, s32[256]{0:T(256)S(1)} %dynamic_update_slice.3, f32[256]{0:T(256)} %param.12, pred[8]{0:T(512)(128)(4,1)S(1)} %get-tuple-element.18, pred[8]{0:T(512)(128)(4,1)S(1)} %get-tuple-element.20, ...), kind=kLoop, calls=%fused_computation.3 | loop fusion | flops 12288 | bytes 16416 | tf_op jit(solution)/shard_map/jit(_where)/select_n | solution.py:452
  2.1 0.0 copy-start
  2.1 0.1 prepare.1
  2.2 0.5 %collective-permute-start = (f32[1,4,256]{2,1,0:T(4,128)S(1)}, f32[1,4,256]{2,1,0:T(4,128)S(1)}, u32[]{:S(2)}, u32[]{:S(2)}) collective-permute-start(f32[1,4,256]{2,1,0:T(4,128)S(1)} %prepare.1), channel_id=1, source_target_pairs={{0,1},{1,0},{2,3},{3,2},{4,5},{5,4},{6,7},{7,6},{8,9},{9,8},{10,11... | collective-permute-start | bytes 12296 | tf_op jit(solution)/shard_map/ppermute | solution.py:525
  2.7 0.0 copy-start.1
  2.7 0.1 broadcast_select_fusion.refs_0_
  2.8 0.4 %hats.1 = (bf16[128,176]{1,0:T(8,128)(2,1)S(1)}, bf16[176,256]{1,0:T(8,128)(2,1)S(1)}, bf16[4,256,128]{2,1,0:T(8,128)(2,1)S(1)}, bf16[4,256,128]{2,1,0:T(8,128)(...) custom-call(), custom_call_target="tpu_custom_call" | custom-call | flops 1500000000 | tf_op jit(solution)/shard_map/hats/pallas_call | solution.py:425
  3.2 0.3 %collective-permute-done = f32[1,4,256]{2,1,0:T(4,128)S(1)} collective-permute-done((f32[1,4,256]{2,1,0:T(4,128)S(1)}, f32[1,4,256]{2,1,0:T(4,128)S(1)}, u32[]{:S(2)}, u32[]{:S(2)}) %collective-permute-start) | collective-permute-done | bytes 4128 | tf_op jit(solution)/shard_map/ppermute | solution.py:525
  3.5 3.7 %collective-permute-start.1 = (f32[2,4,256]{2,1,0:T(4,128)S(1)}, f32[2,4,256]{2,1,0:T(4,128)S(1)}, u32[]{:S(2)}, u32[]{:S(2)}) collective-permute-start(f32[2,4,256]{2,1,0:T(4,128)S(1)} %pad_maximum_fusion.2.refs_5_), channel_id=1, source_target_pairs={{0,9},{1,8},{4,13},{5,12},{8,1},{9,0},{12,5},{13,4},{2,11},{3,10},... | collective-permute-start | bytes 24584 | tf_op jit(solution)/shard_map/ppermute | solution.py:525
  7.2 0.0 copy-done
  7.2 0.0 copy-done.1
  7.2 2.5 %turned.1.refs_3_ = f32[2160,128]{1,0:T(8,128)S(1)} custom-call(f32[64,128,128]{2,1,0:T(8,128)S(1)} %copy-done.1, f32[1,4]{1,0:T(1,128)S(1)} %bitcast.2, bf16[176,256]{1,0:T(8,128)(2,1)S(1)} %get-tuple-element.10.refs_2_, bf16[4,256,128]{2,1,0:T(8,128)(2,1)S(1)} %get-tuple-element.11.refs_3_, bf16[80,512]{1,0:T(8,128)(2,1)S(1)} %get-tuple-element.12.refs_4_, ...), custom_call_target="tpu_custom_call" | custom-call | flops 2000000000 | bytes 4194304 | tf_op jit(solution)/shard_map/turned/pallas_call | solution.py:528
  9.8 0.0 collective-permute-done.1
  9.8 1.5 %collective-permute-start.2 = (f32[4,4,256]{2,1,0:T(4,128)S(1)}, f32[4,4,256]{2,1,0:T(4,128)S(1)}, u32[]{:S(2)}, u32[]{:S(2)}) collective-permute-start(f32[4,4,256]{2,1,0:T(4,128)S(1)} %pad_maximum_fusion.1.refs_1_), channel_id=1, source_target_pairs={{0,3},{1,2},{2,1},{3,0},{4,7},{5,6},{6,5},{7,4},{8,11},{9,10},{10,... | collective-permute-start | bytes 49160 | tf_op jit(solution)/shard_map/ppermute | solution.py:525
  11.3 1.7 %spread.3.refs_2_ = f32[2160,128]{1,0:T(8,128)S(1)} custom-call(f32[8,128]{1,0:T(8,128)S(1)} %broadcast_select_fusion.refs_0_, f32[4,4,256]{2,1,0:T(4,128)S(1)} %pad_maximum_fusion.1.refs_1_), custom_call_target="tpu_custom_call" | custom-call | flops 1132462080 | tf_op jit(solution)/shard_map/spread/pallas_call | solution.py:474
  12.9 0.1 collective-permute-done.2.refs_1_
  13.0 1.6 %collective-permute-start.3 = (f32[8,4,256]{2,1,0:T(4,128)S(1)}, f32[8,4,256]{2,1,0:T(4,128)S(1)}, u32[]{:S(2)}, u32[]{:S(2)}) collective-permute-start(f32[8,4,256]{2,1,0:T(4,128)S(1)} %pad_maximum_fusion), channel_id=1, source_target_pairs={{0,5},{1,4},{4,1},{5,0},{8,13},{9,12},{12,9},{13,8},{2,7},{3,6},{6... | collective-permute-start | bytes 98312 | tf_op jit(solution)/shard_map/ppermute | solution.py:525
  14.6 1.8 %spread.4.refs_2_ = f32[2160,128]{1,0:T(8,128)S(1)} custom-call(f32[8,128]{1,0:T(8,128)S(1)} %broadcast_select_fusion.refs_0_, f32[4,4,256]{2,1,0:T(4,128)S(1)} %collective-permute-done.2.refs_1_, f32[2160,128]{1,0:T(8,128)S(1)} %spread.3.refs_2_), custom_call_target="tpu_custom_call", output_to_operand_aliasing={{}: (2, {})} | custom-call | flops 1132462080 | tf_op jit(solution)/shard_map/spread/pallas_call | solution.py:474
  16.4 0.0 collective-permute-done.3.refs_1_
  16.4 3.3 %spread.5 = (f32[2160,128]{1,0:T(8,128)S(1)}, f32[8,128]{1,0:T(8,128)S(1)}) custom-call(f32[8,128]{1,0:T(8,128)S(1)} %broadcast_select_fusion.refs_0_, f32[8,4,256]{2,1,0:T(4,128)S(1)} %collective-permute-done.3.refs_1_, f32[2160,128]{1,0:T(8,128)S(1)} %spread.4.refs_2_, f32[2160,128]{1,0:T(8,128)S(1)} %turned.1.refs_3_), custom_call_target="tpu_custom_call", output_to_operand_aliasing={{0}: (2, {})} | custom-call | flops 2264924160 | tf_op jit(solution)/shard_map/spread/pallas_call | solution.py:474
  19.7 0.4 %collective-permute-start.4 = (f32[8,128]{1,0:T(8,128)S(1)}, f32[8,128]{1,0:T(8,128)S(1)}, u32[]{:S(2)}, u32[]{:S(2)}) collective-permute-start(f32[8,128]{1,0:T(8,128)S(1)} %get-tuple-element.17), channel_id=1, source_target_pairs={{0,1},{1,0},{2,3},{3,2},{4,5},{5,4},{6,7},{7,6},{8,9},{9,8},{10,11... | collective-permute-start | bytes 12296 | tf_op jit(solution)/shard_map/ppermute | solution.py:557
  20.1 0.8 %collective-permute-done.4 = f32[8,128]{1,0:T(8,128)S(1)} collective-permute-done((f32[8,128]{1,0:T(8,128)S(1)}, f32[8,128]{1,0:T(8,128)S(1)}, u32[]{:S(2)}, u32[]{:S(2)}) %collective-permute-start.4) | collective-permute-done | bytes 4128 | tf_op jit(solution)/shard_map/ppermute | solution.py:557
  20.9 1.4 %collective-permute-start.5 = (f32[8,128]{1,0:T(8,128)S(1)}, f32[8,128]{1,0:T(8,128)S(1)}, u32[]{:S(2)}, u32[]{:S(2)}) collective-permute-start(f32[8,128]{1,0:T(8,128)S(1)} %add.17.refs_5_), channel_id=1, source_target_pairs={{0,9},{1,8},{4,13},{5,12},{8,1},{9,0},{12,5},{13,4},{2,11},{3,10},... | collective-permute-start | bytes 12296 | tf_op jit(solution)/shard_map/ppermute | solution.py:557
  22.3 2.1 %field.3.refs_6_ = f32[64,128,128]{2,1,0:T(8,128)} custom-call(f32[2160,128]{1,0:T(8,128)S(1)} %get-tuple-element.13.refs_0_, f32[1,4]{1,0:T(1,128)S(1)} %bitcast.3, bf16[128,176]{1,0:T(8,128)(2,1)S(1)} %get-tuple-element.14.refs_2_, bf16[4,256,128]{2,1,0:T(8,128)(2,1)S(1)} %get-tuple-element.15.refs_3_, bf16[512,80]{1,0:T(8,128)(2,1)S(1)} %get-tuple-element.16.refs_4_, ...), custom_call_target="tpu_custom_call" | custom-call | flops 1000000000 | bytes 2097152 | tf_op jit(solution)/shard_map/field/pallas_call | solution.py:500
  24.4 0.4 %collective-permute-done.5 = f32[8,128]{1,0:T(8,128)S(1)} collective-permute-done((f32[8,128]{1,0:T(8,128)S(1)}, f32[8,128]{1,0:T(8,128)S(1)}, u32[]{:S(2)}, u32[]{:S(2)}) %collective-permute-start.5) | collective-permute-done | bytes 4128 | tf_op jit(solution)/shard_map/ppermute | solution.py:557
  24.9 1.4 %collective-permute-start.6 = (f32[8,128]{1,0:T(8,128)S(1)}, f32[8,128]{1,0:T(8,128)S(1)}, u32[]{:S(2)}, u32[]{:S(2)}) collective-permute-start(f32[8,128]{1,0:T(8,128)S(1)} %add.18.refs_5_), channel_id=1, source_target_pairs={{0,3},{1,2},{2,1},{3,0},{4,7},{5,6},{6,5},{7,4},{8,11},{9,10},{10,... | collective-permute-start | bytes 12296 | tf_op jit(solution)/shard_map/ppermute | solution.py:557
  26.3 1.6 %field.4.refs_6_ = f32[64,128,128]{2,1,0:T(8,128)} custom-call(f32[2160,128]{1,0:T(8,128)S(1)} %get-tuple-element.13.refs_0_, f32[1,4]{1,0:T(1,128)S(1)} %bitcast.4, bf16[128,176]{1,0:T(8,128)(2,1)S(1)} %get-tuple-element.14.refs_2_, bf16[4,256,128]{2,1,0:T(8,128)(2,1)S(1)} %get-tuple-element.15.refs_3_, ...), custom_call_target="tpu_custom_call", output_to_operand_aliasing={{}: (6, {})} | custom-call | flops 1000000000 | bytes 1048576 | tf_op jit(solution)/shard_map/field/pallas_call | solution.py:500
  27.9 0.0 collective-permute-done.6
  28.0 1.5 %collective-permute-start.7 = (f32[8,128]{1,0:T(8,128)S(1)}, f32[8,128]{1,0:T(8,128)S(1)}, u32[]{:S(2)}, u32[]{:S(2)}) collective-permute-start(f32[8,128]{1,0:T(8,128)S(1)} %add.19.refs_5_.refs_0_), channel_id=1, source_target_pairs={{0,5},{1,4},{4,1},{5,0},{8,13},{9,12},{12,9},{13,8},{2,7},{3,6},{6... | collective-permute-start | bytes 12296 | tf_op jit(solution)/shard_map/ppermute | solution.py:557
  29.4 1.6 %field.5 = f32[64,128,128]{2,1,0:T(8,128)} custom-call(f32[2160,128]{1,0:T(8,128)S(1)} %get-tuple-element.13.refs_0_, f32[1,4]{1,0:T(1,128)S(1)} %bitcast.5, bf16[128,176]{1,0:T(8,128)(2,1)S(1)} %get-tuple-element.14.refs_2_, bf16[4,256,128]{2,1,0:T(8,128)(2,1)S(1)} %get-tuple-element.15.refs_3_, ...), custom_call_target="tpu_custom_call", output_to_operand_aliasing={{}: (6, {})} | custom-call | flops 1000000000 | bytes 1048576 | tf_op jit(solution)/shard_map/field/pallas_call | solution.py:500
  31.1 0.0 collective-permute-done.7.refs_1_
  31.1 0.6 %finish.1 = f32[1,1]{1,0:T(1,128)} custom-call(f32[8,128]{1,0:T(8,128)S(1)} %add.19.refs_5_.refs_0_, f32[8,128]{1,0:T(8,128)S(1)} %collective-permute-done.7.refs_1_), custom_call_target="tpu_custom_call" | custom-call | tf_op jit(solution)/shard_map/finish/pallas_call | solution.py:564
  (10 shorter events, 0.1 us)
Async XLA Ops:
  2.1 5.1 %copy-start = (f32[4]{0:T(128)S(1)}, f32[4]{0:T(128)}, u32[]{:S(2)}) copy-start(f32[4]{0:T(128)} %param.14) | copy-start | bytes 52
  2.2 1.3 %collective-permute-start = (f32[1,4,256]{2,1,0:T(4,128)S(1)}, f32[1,4,256]{2,1,0:T(4,128)S(1)}, u32[]{:S(2)}, u32[]{:S(2)}) collective-permute-start(f32[1,4,256]{2,1,0:T(4,128)S(1)} %prepare.1), channel_id=1, source_target_pairs={{0,1},{1,0},{2,3},{3,2},{4,5},{5,4},{6,7},{7,6},{8,9},{9,8},{10,11... | collective-permute-start | bytes 12296 | tf_op jit(solution)/shard_map/ppermute | solution.py:525
  2.7 4.5 %copy-start.1 = (f32[64,128,128]{2,1,0:T(8,128)S(1)}, f32[64,128,128]{2,1,0:T(8,128)}, u32[]{:S(2)}) copy-start(f32[64,128,128]{2,1,0:T(8,128)} %refs_0_.1) | copy-start | bytes 12582916
  3.5 6.2 %collective-permute-start.1 = (f32[2,4,256]{2,1,0:T(4,128)S(1)}, f32[2,4,256]{2,1,0:T(4,128)S(1)}, u32[]{:S(2)}, u32[]{:S(2)}) collective-permute-start(f32[2,4,256]{2,1,0:T(4,128)S(1)} %pad_maximum_fusion.2.refs_5_), channel_id=1, source_target_pairs={{0,9},{1,8},{4,13},{5,12},{8,1},{9,0},{12,5},{13,4},{2,11},{3,10},... | collective-permute-start | bytes 24584 | tf_op jit(solution)/shard_map/ppermute | solution.py:525
  9.8 3.2 %collective-permute-start.2 = (f32[4,4,256]{2,1,0:T(4,128)S(1)}, f32[4,4,256]{2,1,0:T(4,128)S(1)}, u32[]{:S(2)}, u32[]{:S(2)}) collective-permute-start(f32[4,4,256]{2,1,0:T(4,128)S(1)} %pad_maximum_fusion.1.refs_1_), channel_id=1, source_target_pairs={{0,3},{1,2},{2,1},{3,0},{4,7},{5,6},{6,5},{7,4},{8,11},{9,10},{10,... | collective-permute-start | bytes 49160 | tf_op jit(solution)/shard_map/ppermute | solution.py:525
  13.0 3.4 %collective-permute-start.3 = (f32[8,4,256]{2,1,0:T(4,128)S(1)}, f32[8,4,256]{2,1,0:T(4,128)S(1)}, u32[]{:S(2)}, u32[]{:S(2)}) collective-permute-start(f32[8,4,256]{2,1,0:T(4,128)S(1)} %pad_maximum_fusion), channel_id=1, source_target_pairs={{0,5},{1,4},{4,1},{5,0},{8,13},{9,12},{12,9},{13,8},{2,7},{3,6},{6... | collective-permute-start | bytes 98312 | tf_op jit(solution)/shard_map/ppermute | solution.py:525
  19.7 1.2 %collective-permute-start.4 = (f32[8,128]{1,0:T(8,128)S(1)}, f32[8,128]{1,0:T(8,128)S(1)}, u32[]{:S(2)}, u32[]{:S(2)}) collective-permute-start(f32[8,128]{1,0:T(8,128)S(1)} %get-tuple-element.17), channel_id=1, source_target_pairs={{0,1},{1,0},{2,3},{3,2},{4,5},{5,4},{6,7},{7,6},{8,9},{9,8},{10,11... | collective-permute-start | bytes 12296 | tf_op jit(solution)/shard_map/ppermute | solution.py:557
  20.9 3.9 %collective-permute-start.5 = (f32[8,128]{1,0:T(8,128)S(1)}, f32[8,128]{1,0:T(8,128)S(1)}, u32[]{:S(2)}, u32[]{:S(2)}) collective-permute-start(f32[8,128]{1,0:T(8,128)S(1)} %add.17.refs_5_), channel_id=1, source_target_pairs={{0,9},{1,8},{4,13},{5,12},{8,1},{9,0},{12,5},{13,4},{2,11},{3,10},... | collective-permute-start | bytes 12296 | tf_op jit(solution)/shard_map/ppermute | solution.py:557
  24.9 3.1 %collective-permute-start.6 = (f32[8,128]{1,0:T(8,128)S(1)}, f32[8,128]{1,0:T(8,128)S(1)}, u32[]{:S(2)}, u32[]{:S(2)}) collective-permute-start(f32[8,128]{1,0:T(8,128)S(1)} %add.18.refs_5_), channel_id=1, source_target_pairs={{0,3},{1,2},{2,1},{3,0},{4,7},{5,6},{6,5},{7,4},{8,11},{9,10},{10,... | collective-permute-start | bytes 12296 | tf_op jit(solution)/shard_map/ppermute | solution.py:557
  28.0 3.1 %collective-permute-start.7 = (f32[8,128]{1,0:T(8,128)S(1)}, f32[8,128]{1,0:T(8,128)S(1)}, u32[]{:S(2)}, u32[]{:S(2)}) collective-permute-start(f32[8,128]{1,0:T(8,128)S(1)} %add.19.refs_5_.refs_0_), channel_id=1, source_target_pairs={{0,5},{1,4},{4,1},{5,0},{8,13},{9,12},{12,9},{13,8},{2,7},{3,6},{6... | collective-permute-start | bytes 12296 | tf_op jit(solution)/shard_map/ppermute | solution.py:557

commit v4 on v3

--- a/solution.py
+++ b/solution.py
@@ -16,6 +16,7 @@
 GROUPS = ((0, 1), (2, 3))
 
 
+SIZES = (3, 5)
 SHARES = (0, 0.5, 0.25, 0.25)
 
 spread_width = 1.25
@@ -197,7 +198,7 @@
     return value[0]
 
 
-def spread_kernel(plan, together, first, last, *refs):
+def spread_kernel(plan, sizes, first, last, *refs):
     refs = list(refs)
     index, charges = refs[:2]
     before = None if first else refs[2]
@@ -207,11 +208,9 @@
         energy = outs.pop(1)
     grids, along_x, along_y, along_z, planes = outs
     begin = [index[axis : axis + 1, :1] for axis in range(3)]
-    steps = charges.shape[0] // together
-
-    def one_step(step, before):
+    def one_step(start, together, before):
         for number in range(together):
-            block = charges[step * together + number]
+            block = charges[start + number]
             columns = slice(number * BQ, (number + 1) * BQ)
             weighted, place_x, place_y, place_z = (block[row : row + 1] for row in range(4))
             for group, levels in enumerate(GROUPS):
@@ -255,15 +254,18 @@
             for rows in [plan.main(level, 0, plan.nodes_x[level]) for level in levels] + [
                 slice(at, at + plan.edge_rows[group])
             ]:
-                value = dot(planes[rows], along_z[group], transposed=True)
+                deep = together * BQ
+                value = dot(planes[rows, :deep], along_z[group, :, :deep], transposed=True)
                 grids[rows] = value if before is None else before[rows] + value
 
-    one_step(0, before)
-    if steps <= 2:
-        for step in range(1, steps):
-            one_step(step, grids)
-    else:
-        lax.fori_loop(1, steps, lambda step, _: one_step(step, grids), None)
+    count = sum(sizes)
+    for number, size in enumerate(sizes):
+        one_step(sum(sizes[:number]), size, grids if number else before)
+    rest = (charges.shape[0] - count) // sizes[-1]
+    if rest:
+        lax.fori_loop(
+            0, rest, lambda step, _: one_step(count + step * sizes[-1], sizes[-1], grids), None
+        )
     if last:
         energy[...] = fold((grids[...] * turned[...]).reshape(-1, 8, plan.width))
 
@@ -467,12 +469,12 @@
 
     def spread(charges, before, turned):
         count = charges.shape[0]
-        together = math.gcd(count, 4)
-        deep = together * BQ
+        sizes = SIZES if count == 8 else (math.gcd(count, 4),)
+        deep = max(sizes) * BQ
         first, last = before is None, turned is not None
         operands = [begin, charges] + [x for x in (before, turned) if x is not None]
         return pl.pallas_call(
-            lambda *refs: spread_kernel(plan, together, first, last, *refs),
+            lambda *refs: spread_kernel(plan, sizes, first, last, *refs),
             out_shape=[grid_shape] + [jax.ShapeDtypeStruct((8, plan.width), f32)] * last,
             in_specs=[vmem] * len(operands),
             out_specs=[vmem] * (1 + last),

time: 31.8 us -> 31.8 us (level)
  no operation moved by 1% of the time
where the time goes in v4:
time: 31.8 us; the launch traced here: 31.6 us
  Pallas kernels  15.7 us (49%)
  starting transfers between devices  11.8 us (37%)
  waiting for transfers between devices  1.72 us (5%)
  between operations  1.41 us (4%)
  other arithmetic  0.95 us (3%)
    ppermute x4, starting transfers between devices, on_device(): got = lax.ppermute(held, axis, pairs)  7.23 us
    pallas_call x3, Pallas kernels, spread(): pl.pallas_call(lambda *refs: spread_kernel(plan, sizes, first, last, *ref...  6.71 us
    pallas_call x3, Pallas kernels, draw(): pl.pallas_call(lambda *refs: field_kernel(plan, planes, chunk, *refs), ou...  5.38 us
    ppermute x4, starting transfers between devices, on_device(): got = lax.ppermute(energy, axis, pairs)  4.6 us
    pallas_call x1, Pallas kernels, on_device(): pl.pallas_call(lambda *refs: turned_kernel(plan, *refs), out_shape=grid_s...  2.54 us
    ppermute x4, waiting for transfers between devices, on_device(): got = lax.ppermute(energy, axis, pairs)  1.31 us
    select_n x1, other arithmetic, on_device(): raw = jnp.where(row == 0, charge[None], raw)  0.82 us
  transfers between devices with their start and end apart: 8, of which 4 were waited for; matrix products, arithmetic and copies ran while one was open for 0% of the time, Pallas kernels for 37%

profile of v4, /device:TPU:0, one launch (start us, length us, event | category | flops | bytes accessed | tf_op | source)
XLA Modules:
  0.0 31.6 jit_solution(16743528093228999093)
XLA Ops:
  1.3 0.8 %add_select_fusion.raw = f32[8,256]{1,0:T(8,128)S(1)} fusion(f32[3,256]{1,0:T(4,128)} %param.11, s32[256]{0:T(256)} %param.10, s32[256]{0:T(256)} %param.9, s32[256]{0:T(256)} %param.8, s32[256]{0:T(256)S(1)} %dynamic_update_slice.3, f32[256]{0:T(256)} %param.12, pred[8]{0:T(512)(128)(4,1)S(1)} %get-tuple-element.18, pred[8]{0:T(512)(128)(4,1)S(1)} %get-tuple-element.20, ...), kind=kLoop, calls=%fused_computation.3 | loop fusion | flops 12288 | bytes 16416 | tf_op jit(solution)/shard_map/jit(_where)/select_n | solution.py:454
  2.1 0.0 copy-start
  2.1 0.1 prepare.1
  2.2 0.5 %collective-permute-start = (f32[1,4,256]{2,1,0:T(4,128)S(1)}, f32[1,4,256]{2,1,0:T(4,128)S(1)}, u32[]{:S(2)}, u32[]{:S(2)}) collective-permute-start(f32[1,4,256]{2,1,0:T(4,128)S(1)} %prepare.1), channel_id=1, source_target_pairs={{0,1},{1,0},{2,3},{3,2},{4,5},{5,4},{6,7},{7,6},{8,9},{9,8},{10,11... | collective-permute-start | bytes 12296 | tf_op jit(solution)/shard_map/ppermute | solution.py:527
  2.7 0.0 copy-start.1
  2.7 0.1 broadcast_select_fusion.refs_0_
  2.8 0.4 %hats.1 = (bf16[128,176]{1,0:T(8,128)(2,1)S(1)}, bf16[176,256]{1,0:T(8,128)(2,1)S(1)}, bf16[4,256,128]{2,1,0:T(8,128)(2,1)S(1)}, bf16[4,256,128]{2,1,0:T(8,128)(...) custom-call(), custom_call_target="tpu_custom_call" | custom-call | flops 1500000000 | tf_op jit(solution)/shard_map/hats/pallas_call | solution.py:427
  3.2 0.3 %collective-permute-done = f32[1,4,256]{2,1,0:T(4,128)S(1)} collective-permute-done((f32[1,4,256]{2,1,0:T(4,128)S(1)}, f32[1,4,256]{2,1,0:T(4,128)S(1)}, u32[]{:S(2)}, u32[]{:S(2)}) %collective-permute-start) | collective-permute-done | bytes 4128 | tf_op jit(solution)/shard_map/ppermute | solution.py:527
  3.5 3.7 %collective-permute-start.1 = (f32[2,4,256]{2,1,0:T(4,128)S(1)}, f32[2,4,256]{2,1,0:T(4,128)S(1)}, u32[]{:S(2)}, u32[]{:S(2)}) collective-permute-start(f32[2,4,256]{2,1,0:T(4,128)S(1)} %pad_maximum_fusion.2.refs_5_), channel_id=1, source_target_pairs={{0,9},{1,8},{4,13},{5,12},{8,1},{9,0},{12,5},{13,4},{2,11},{3,10},... | collective-permute-start | bytes 24584 | tf_op jit(solution)/shard_map/ppermute | solution.py:527
  7.2 0.0 copy-done
  7.2 0.0 copy-done.1
  7.2 2.5 %turned.1.refs_3_ = f32[2160,128]{1,0:T(8,128)S(1)} custom-call(f32[64,128,128]{2,1,0:T(8,128)S(1)} %copy-done.1, f32[1,4]{1,0:T(1,128)S(1)} %bitcast.2, bf16[176,256]{1,0:T(8,128)(2,1)S(1)} %get-tuple-element.10.refs_2_, bf16[4,256,128]{2,1,0:T(8,128)(2,1)S(1)} %get-tuple-element.11.refs_3_, bf16[80,512]{1,0:T(8,128)(2,1)S(1)} %get-tuple-element.12.refs_4_, ...), custom_call_target="tpu_custom_call" | custom-call | flops 2000000000 | bytes 4194304 | tf_op jit(solution)/shard_map/turned/pallas_call | solution.py:530
  9.8 0.0 collective-permute-done.1
  9.8 1.5 %collective-permute-start.2 = (f32[4,4,256]{2,1,0:T(4,128)S(1)}, f32[4,4,256]{2,1,0:T(4,128)S(1)}, u32[]{:S(2)}, u32[]{:S(2)}) collective-permute-start(f32[4,4,256]{2,1,0:T(4,128)S(1)} %pad_maximum_fusion.1.refs_1_), channel_id=1, source_target_pairs={{0,3},{1,2},{2,1},{3,0},{4,7},{5,6},{6,5},{7,4},{8,11},{9,10},{10,... | collective-permute-start | bytes 49160 | tf_op jit(solution)/shard_map/ppermute | solution.py:527
  11.3 1.7 %spread.3.refs_2_ = f32[2160,128]{1,0:T(8,128)S(1)} custom-call(f32[8,128]{1,0:T(8,128)S(1)} %broadcast_select_fusion.refs_0_, f32[4,4,256]{2,1,0:T(4,128)S(1)} %pad_maximum_fusion.1.refs_1_), custom_call_target="tpu_custom_call" | custom-call | flops 1132462080 | tf_op jit(solution)/shard_map/spread/pallas_call | solution.py:476
  12.9 0.1 collective-permute-done.2.refs_1_
  13.0 1.6 %collective-permute-start.3 = (f32[8,4,256]{2,1,0:T(4,128)S(1)}, f32[8,4,256]{2,1,0:T(4,128)S(1)}, u32[]{:S(2)}, u32[]{:S(2)}) collective-permute-start(f32[8,4,256]{2,1,0:T(4,128)S(1)} %pad_maximum_fusion), channel_id=1, source_target_pairs={{0,5},{1,4},{4,1},{5,0},{8,13},{9,12},{12,9},{13,8},{2,7},{3,6},{6... | collective-permute-start | bytes 98312 | tf_op jit(solution)/shard_map/ppermute | solution.py:527
  14.6 1.8 %spread.4.refs_2_ = f32[2160,128]{1,0:T(8,128)S(1)} custom-call(f32[8,128]{1,0:T(8,128)S(1)} %broadcast_select_fusion.refs_0_, f32[4,4,256]{2,1,0:T(4,128)S(1)} %collective-permute-done.2.refs_1_, f32[2160,128]{1,0:T(8,128)S(1)} %spread.3.refs_2_), custom_call_target="tpu_custom_call", output_to_operand_aliasing={{}: (2, {})} | custom-call | flops 1132462080 | tf_op jit(solution)/shard_map/spread/pallas_call | solution.py:476
  16.4 0.0 collective-permute-done.3.refs_1_
  16.4 3.2 %spread.5 = (f32[2160,128]{1,0:T(8,128)S(1)}, f32[8,128]{1,0:T(8,128)S(1)}) custom-call(f32[8,128]{1,0:T(8,128)S(1)} %broadcast_select_fusion.refs_0_, f32[8,4,256]{2,1,0:T(4,128)S(1)} %collective-permute-done.3.refs_1_, f32[2160,128]{1,0:T(8,128)S(1)} %spread.4.refs_2_, f32[2160,128]{1,0:T(8,128)S(1)} %turned.1.refs_3_), custom_call_target="tpu_custom_call", output_to_operand_aliasing={{0}: (2, {})} | custom-call | flops 2264924160 | tf_op jit(solution)/shard_map/spread/pallas_call | solution.py:476
  19.7 0.4 %collective-permute-start.4 = (f32[8,128]{1,0:T(8,128)S(1)}, f32[8,128]{1,0:T(8,128)S(1)}, u32[]{:S(2)}, u32[]{:S(2)}) collective-permute-start(f32[8,128]{1,0:T(8,128)S(1)} %get-tuple-element.17), channel_id=1, source_target_pairs={{0,1},{1,0},{2,3},{3,2},{4,5},{5,4},{6,7},{7,6},{8,9},{9,8},{10,11... | collective-permute-start | bytes 12296 | tf_op jit(solution)/shard_map/ppermute | solution.py:559
  20.0 0.9 %collective-permute-done.4 = f32[8,128]{1,0:T(8,128)S(1)} collective-permute-done((f32[8,128]{1,0:T(8,128)S(1)}, f32[8,128]{1,0:T(8,128)S(1)}, u32[]{:S(2)}, u32[]{:S(2)}) %collective-permute-start.4) | collective-permute-done | bytes 4128 | tf_op jit(solution)/shard_map/ppermute | solution.py:559
  20.9 1.4 %collective-permute-start.5 = (f32[8,128]{1,0:T(8,128)S(1)}, f32[8,128]{1,0:T(8,128)S(1)}, u32[]{:S(2)}, u32[]{:S(2)}) collective-permute-start(f32[8,128]{1,0:T(8,128)S(1)} %add.17.refs_5_), channel_id=1, source_target_pairs={{0,9},{1,8},{4,13},{5,12},{8,1},{9,0},{12,5},{13,4},{2,11},{3,10},... | collective-permute-start | bytes 12296 | tf_op jit(solution)/shard_map/ppermute | solution.py:559
  22.3 2.1 %field.3.refs_6_ = f32[64,128,128]{2,1,0:T(8,128)} custom-call(f32[2160,128]{1,0:T(8,128)S(1)} %get-tuple-element.13.refs_0_, f32[1,4]{1,0:T(1,128)S(1)} %bitcast.3, bf16[128,176]{1,0:T(8,128)(2,1)S(1)} %get-tuple-element.14.refs_2_, bf16[4,256,128]{2,1,0:T(8,128)(2,1)S(1)} %get-tuple-element.15.refs_3_, bf16[512,80]{1,0:T(8,128)(2,1)S(1)} %get-tuple-element.16.refs_4_, ...), custom_call_target="tpu_custom_call" | custom-call | flops 1000000000 | bytes 2097152 | tf_op jit(solution)/shard_map/field/pallas_call | solution.py:502
  24.4 0.4 %collective-permute-done.5 = f32[8,128]{1,0:T(8,128)S(1)} collective-permute-done((f32[8,128]{1,0:T(8,128)S(1)}, f32[8,128]{1,0:T(8,128)S(1)}, u32[]{:S(2)}, u32[]{:S(2)}) %collective-permute-start.5) | collective-permute-done | bytes 4128 | tf_op jit(solution)/shard_map/ppermute | solution.py:559
  24.8 1.4 %collective-permute-start.6 = (f32[8,128]{1,0:T(8,128)S(1)}, f32[8,128]{1,0:T(8,128)S(1)}, u32[]{:S(2)}, u32[]{:S(2)}) collective-permute-start(f32[8,128]{1,0:T(8,128)S(1)} %add.18.refs_5_), channel_id=1, source_target_pairs={{0,3},{1,2},{2,1},{3,0},{4,7},{5,6},{6,5},{7,4},{8,11},{9,10},{10,... | collective-permute-start | bytes 12296 | tf_op jit(solution)/shard_map/ppermute | solution.py:559
  26.2 1.6 %field.4.refs_6_ = f32[64,128,128]{2,1,0:T(8,128)} custom-call(f32[2160,128]{1,0:T(8,128)S(1)} %get-tuple-element.13.refs_0_, f32[1,4]{1,0:T(1,128)S(1)} %bitcast.4, bf16[128,176]{1,0:T(8,128)(2,1)S(1)} %get-tuple-element.14.refs_2_, bf16[4,256,128]{2,1,0:T(8,128)(2,1)S(1)} %get-tuple-element.15.refs_3_, ...), custom_call_target="tpu_custom_call", output_to_operand_aliasing={{}: (6, {})} | custom-call | flops 1000000000 | bytes 1048576 | tf_op jit(solution)/shard_map/field/pallas_call | solution.py:502
  27.9 0.0 collective-permute-done.6
  27.9 1.5 %collective-permute-start.7 = (f32[8,128]{1,0:T(8,128)S(1)}, f32[8,128]{1,0:T(8,128)S(1)}, u32[]{:S(2)}, u32[]{:S(2)}) collective-permute-start(f32[8,128]{1,0:T(8,128)S(1)} %add.19.refs_5_.refs_0_), channel_id=1, source_target_pairs={{0,5},{1,4},{4,1},{5,0},{8,13},{9,12},{12,9},{13,8},{2,7},{3,6},{6... | collective-permute-start | bytes 12296 | tf_op jit(solution)/shard_map/ppermute | solution.py:559
  29.4 1.6 %field.5 = f32[64,128,128]{2,1,0:T(8,128)} custom-call(f32[2160,128]{1,0:T(8,128)S(1)} %get-tuple-element.13.refs_0_, f32[1,4]{1,0:T(1,128)S(1)} %bitcast.5, bf16[128,176]{1,0:T(8,128)(2,1)S(1)} %get-tuple-element.14.refs_2_, bf16[4,256,128]{2,1,0:T(8,128)(2,1)S(1)} %get-tuple-element.15.refs_3_, ...), custom_call_target="tpu_custom_call", output_to_operand_aliasing={{}: (6, {})} | custom-call | flops 1000000000 | bytes 1048576 | tf_op jit(solution)/shard_map/field/pallas_call | solution.py:502
  31.0 0.0 collective-permute-done.7.refs_1_
  31.0 0.6 %finish.1 = f32[1,1]{1,0:T(1,128)} custom-call(f32[8,128]{1,0:T(8,128)S(1)} %add.19.refs_5_.refs_0_, f32[8,128]{1,0:T(8,128)S(1)} %collective-permute-done.7.refs_1_), custom_call_target="tpu_custom_call" | custom-call | tf_op jit(solution)/shard_map/finish/pallas_call | solution.py:566
  (10 shorter events, 0.1 us)
Async XLA Ops:
  2.1 5.1 %copy-start = (f32[4]{0:T(128)S(1)}, f32[4]{0:T(128)}, u32[]{:S(2)}) copy-start(f32[4]{0:T(128)} %param.14) | copy-start | bytes 52
  2.2 1.3 %collective-permute-start = (f32[1,4,256]{2,1,0:T(4,128)S(1)}, f32[1,4,256]{2,1,0:T(4,128)S(1)}, u32[]{:S(2)}, u32[]{:S(2)}) collective-permute-start(f32[1,4,256]{2,1,0:T(4,128)S(1)} %prepare.1), channel_id=1, source_target_pairs={{0,1},{1,0},{2,3},{3,2},{4,5},{5,4},{6,7},{7,6},{8,9},{9,8},{10,11... | collective-permute-start | bytes 12296 | tf_op jit(solution)/shard_map/ppermute | solution.py:527
  2.7 4.5 %copy-start.1 = (f32[64,128,128]{2,1,0:T(8,128)S(1)}, f32[64,128,128]{2,1,0:T(8,128)}, u32[]{:S(2)}) copy-start(f32[64,128,128]{2,1,0:T(8,128)} %refs_0_.1) | copy-start | bytes 12582916
  3.5 6.2 %collective-permute-start.1 = (f32[2,4,256]{2,1,0:T(4,128)S(1)}, f32[2,4,256]{2,1,0:T(4,128)S(1)}, u32[]{:S(2)}, u32[]{:S(2)}) collective-permute-start(f32[2,4,256]{2,1,0:T(4,128)S(1)} %pad_maximum_fusion.2.refs_5_), channel_id=1, source_target_pairs={{0,9},{1,8},{4,13},{5,12},{8,1},{9,0},{12,5},{13,4},{2,11},{3,10},... | collective-permute-start | bytes 24584 | tf_op jit(solution)/shard_map/ppermute | solution.py:527
  9.8 3.2 %collective-permute-start.2 = (f32[4,4,256]{2,1,0:T(4,128)S(1)}, f32[4,4,256]{2,1,0:T(4,128)S(1)}, u32[]{:S(2)}, u32[]{:S(2)}) collective-permute-start(f32[4,4,256]{2,1,0:T(4,128)S(1)} %pad_maximum_fusion.1.refs_1_), channel_id=1, source_target_pairs={{0,3},{1,2},{2,1},{3,0},{4,7},{5,6},{6,5},{7,4},{8,11},{9,10},{10,... | collective-permute-start | bytes 49160 | tf_op jit(solution)/shard_map/ppermute | solution.py:527
  13.0 3.4 %collective-permute-start.3 = (f32[8,4,256]{2,1,0:T(4,128)S(1)}, f32[8,4,256]{2,1,0:T(4,128)S(1)}, u32[]{:S(2)}, u32[]{:S(2)}) collective-permute-start(f32[8,4,256]{2,1,0:T(4,128)S(1)} %pad_maximum_fusion), channel_id=1, source_target_pairs={{0,5},{1,4},{4,1},{5,0},{8,13},{9,12},{12,9},{13,8},{2,7},{3,6},{6... | collective-permute-start | bytes 98312 | tf_op jit(solution)/shard_map/ppermute | solution.py:527
  19.7 1.2 %collective-permute-start.4 = (f32[8,128]{1,0:T(8,128)S(1)}, f32[8,128]{1,0:T(8,128)S(1)}, u32[]{:S(2)}, u32[]{:S(2)}) collective-permute-start(f32[8,128]{1,0:T(8,128)S(1)} %get-tuple-element.17), channel_id=1, source_target_pairs={{0,1},{1,0},{2,3},{3,2},{4,5},{5,4},{6,7},{7,6},{8,9},{9,8},{10,11... | collective-permute-start | bytes 12296 | tf_op jit(solution)/shard_map/ppermute | solution.py:559
  20.9 3.9 %collective-permute-start.5 = (f32[8,128]{1,0:T(8,128)S(1)}, f32[8,128]{1,0:T(8,128)S(1)}, u32[]{:S(2)}, u32[]{:S(2)}) collective-permute-start(f32[8,128]{1,0:T(8,128)S(1)} %add.17.refs_5_), channel_id=1, source_target_pairs={{0,9},{1,8},{4,13},{5,12},{8,1},{9,0},{12,5},{13,4},{2,11},{3,10},... | collective-permute-start | bytes 12296 | tf_op jit(solution)/shard_map/ppermute | solution.py:559
  24.8 3.0 %collective-permute-start.6 = (f32[8,128]{1,0:T(8,128)S(1)}, f32[8,128]{1,0:T(8,128)S(1)}, u32[]{:S(2)}, u32[]{:S(2)}) collective-permute-start(f32[8,128]{1,0:T(8,128)S(1)} %add.18.refs_5_), channel_id=1, source_target_pairs={{0,3},{1,2},{2,1},{3,0},{4,7},{5,6},{6,5},{7,4},{8,11},{9,10},{10,... | collective-permute-start | bytes 12296 | tf_op jit(solution)/shard_map/ppermute | solution.py:559
  27.9 3.1 %collective-permute-start.7 = (f32[8,128]{1,0:T(8,128)S(1)}, f32[8,128]{1,0:T(8,128)S(1)}, u32[]{:S(2)}, u32[]{:S(2)}) collective-permute-start(f32[8,128]{1,0:T(8,128)S(1)} %add.19.refs_5_.refs_0_), channel_id=1, source_target_pairs={{0,5},{1,4},{4,1},{5,0},{8,13},{9,12},{12,9},{13,8},{2,7},{3,6},{6... | collective-permute-start | bytes 12296 | tf_op jit(solution)/shard_map/ppermute | solution.py:559
